TPU v7x, 512 devices: a whole 4x8x8 slice. The times are simulated.
512 devices in a mesh: src: 8 (over x, y_lo), gx: 16 (over z, core), gy: 4 (over y_hi).
Axes of the slice: x: 4, y: 8 (y_hi: 4, y_lo: 2; y = y_hi * 2 + y_lo), z: 8, core: 2. Of those that a mesh axis runs over, the one named last changes fastest.
Arguments:
- warm_potential: float32 [32, 64, 128, 128], P('src', 'gx', 'gy'), may hold values from -3 to 3
- warm_adjoint: float32 [32, 64, 128, 128], P('src', 'gx', 'gy'), may hold values from -3 to 3
- conductivity: float32 [64, 128, 128], P('gx', 'gy', 'src'), may hold values from 0.2 to 5
- electrodes: int32 [32, 2], replicated, may hold values from 0 to 8191
- receivers: int32 [128, 2], replicated, may hold values from 0 to 8191
- observed: float32 [32, 128], replicated, may hold values from -6 to 6
- source_order: int32 [32], replicated, may hold values from 0 to 31, each once
Outputs:
- gradient: float32 [64, 128, 128], P('gx', 'gy', 'src')
Inputs may be any that keep to these rules, and one draw needn't show every extreme that they name: `electrodes`: entries number surface cells as x * 128 + y. `receivers`: entries number surface cells as x * 128 + y.
All inputs are finite; a program needn't handle non-finite values.
Results may differ from a plain program's by a relative error of at most 0.0003.
Values sent between devices are 32-bit elements; how exact they have to be, the bound alone decides.
A program may use at most 64 MiB of HBM per device.

v0:
```python
import jax
import jax.numpy as jnp
from jax import lax
from jax.sharding import PartitionSpec as P

SWEEPS = 6
lowest = 0.05
highest = 2.0
centre = (highest + lowest) / 2.0
half_span = (highest - lowest) / 2.0
bound_ratio = centre / half_span
strength = 4.0


def padded_2(block, sides, width):
    for axis, dim in sides:
        count = lax.axis_size(axis)
        forward = [(i, i + 1) for i in range(count - 1)]
        backward = [(target, source) for source, target in forward]
        low = lax.ppermute(
            lax.slice_in_dim(block, block.shape[dim] - width, None, axis=dim), axis, forward
        )
        high = lax.ppermute(lax.slice_in_dim(block, 0, width, axis=dim), axis, backward)
        block = jnp.concatenate([low, block, high], axis=dim)
    return block


def harmonic(left, right):
    return jnp.where(right > 0, 2.0 * left * right / (left + right), left)


def slope_of(left, right):
    total = left + right
    return jnp.where(right > 0, 2.0 * right * right / (total * total), 1.0)


def neighbours(field, padded):
    widths = [(0, 0)] * (field.ndim - 1) + [(1, 1)]
    deeper = jnp.pad(field, widths)
    return (
        padded[..., :-2, 1:-1, :],
        padded[..., 2:, 1:-1, :],
        padded[..., 1:-1, :-2, :],
        padded[..., 1:-1, 2:, :],
        deeper[..., :-2],
        deeper[..., 2:],
    )


def face_tables(sigma, padded):
    others = neighbours(sigma, padded)
    depth = lax.broadcasted_iota(jnp.int32, sigma.shape, 2)
    surface = depth == 0
    coeffs = [harmonic(sigma, other) for other in others]
    slopes = [slope_of(sigma, other) for other in others]
    coeffs[4] = jnp.where(surface, 0.0, coeffs[4])
    slopes[4] = jnp.where(surface, 0.0, slopes[4])
    return (coeffs, slopes)


def apply_operator(field, padded, coeffs):
    others = neighbours(field, padded)
    total = coeffs[0] * (field - others[0])
    for index in range(1, 6):
        total = total + coeffs[index] * (field - others[index])
    return total


def solve(rhs, start, coeffs, inverse, pad_fn):
    residual = rhs - apply_operator(start, pad_fn(start), coeffs)
    update = inverse * residual / centre
    iterate = start
    factor = 1.0 / bound_ratio
    for sweep in range(SWEEPS):
        iterate = iterate + update
        residual = residual - apply_operator(update, pad_fn(update), coeffs)
        following = 1.0 / (2.0 * bound_ratio - factor)
        update = following * factor * update + 2.0 * following / half_span * (inverse * residual)
        factor = following
    return iterate + update


def gradient_term(potential, adjoint, padded_potential, padded_adjoint, slopes):
    near_potential = neighbours(potential, padded_potential)
    near_adjoint = neighbours(adjoint, padded_adjoint)
    total = slopes[0] * (potential - near_potential[0]) * (adjoint - near_adjoint[0])
    for index in range(1, 6):
        total = total + slopes[index] * (potential - near_potential[index]) * (
            adjoint - near_adjoint[index]
        )
    return total


def pad_joint(field):
    return padded_2(field, (("gx", 1), ("gy", 2)), 1)


def reduce_groups(partial_value, depth):
    summed = lax.psum(partial_value, "src")
    return lax.dynamic_slice_in_dim(summed, lax.axis_index("src") * depth, depth, 2)


def body(warm_potential, warm_adjoint, conductivity, electrodes, receivers, observed, source_order):
    panel = lax.all_gather(conductivity, "src", axis=2, tiled=True)
    group = lax.axis_index("src")
    slots = warm_potential.shape[0]
    width_x = panel.shape[0]
    ny_global = panel.shape[1] * lax.axis_size("gy")
    x_start = lax.axis_index("gx") * width_x
    potential_start, adjoint_start = (warm_potential, warm_adjoint)
    first_slot = group * slots
    y_start = lax.axis_index("gy") * panel.shape[1]
    width_y = panel.shape[1]
    depth_cells = panel.shape[2]
    coeffs, slopes = face_tables(panel, pad_joint(panel[None])[0])
    inverse = 1.0 / (coeffs[0] + coeffs[1] + coeffs[2] + coeffs[3] + coeffs[4] + coeffs[5])
    idents = lax.dynamic_slice_in_dim(source_order, first_slot, slots)
    pairs = jnp.take(electrodes, idents, axis=0)
    rows_observed = jnp.take(observed, idents, axis=0)

    def picker(cells):
        local_x = cells // ny_global - x_start
        local_y = cells % ny_global - y_start
        inside = (local_x >= 0) & (local_x < width_x) & (local_y >= 0) & (local_y < width_y)
        flat = local_x * width_y + local_y
        places = lax.broadcasted_iota(jnp.int32, (cells.shape[0], width_x * width_y), 1)
        return jnp.where((flat[:, None] == places) & inside[:, None], 1.0, 0.0).astype(jnp.float32)

    def on_surface(flat):
        field = jnp.zeros((slots, width_x, width_y, depth_cells), jnp.float32)
        return field.at[..., 0].set(flat.reshape(slots, width_x, width_y))

    source_surface = strength * (picker(pairs[:, 0]) - picker(pairs[:, 1]))
    potential = solve(on_surface(source_surface), potential_start, coeffs, inverse, pad_joint)
    pickup = picker(receivers[:, 0]) - picker(receivers[:, 1])
    top = potential[..., 0].reshape(slots, width_x * width_y)
    local_values = jnp.dot(
        top, pickup.T, precision=lax.Precision.HIGHEST, preferred_element_type=jnp.float32
    )
    predicted = lax.psum(local_values, ("gx", "gy"))
    misfit = predicted - rows_observed
    back = jnp.dot(
        misfit, pickup, precision=lax.Precision.HIGHEST, preferred_element_type=jnp.float32
    )
    adjoint = solve(on_surface(back), adjoint_start, coeffs, inverse, pad_joint)
    padded_both = pad_joint(jnp.concatenate([potential, adjoint], 0))
    term = gradient_term(potential, adjoint, padded_both[:slots], padded_both[slots:], slopes)
    partial_value = -jnp.sum(term, axis=0)
    return reduce_groups(partial_value, conductivity.shape[2])


def solution(mesh):
    in_specs = (
        P("src", "gx", "gy", None),
        P("src", "gx", "gy", None),
        P("gx", "gy", "src"),
        P(),
        P(),
        P(),
        P(),
    )
    out_specs = P("gx", "gy", "src")
    return jax.shard_map(body, mesh=mesh, in_specs=in_specs, out_specs=out_specs, check_vma=False)
```

profile of v0, /device:TPU:16, one launch (start us, length us, event | category | flops | bytes accessed | tf_op | source)
XLA Modules:
  0.0 592.4 jit_solution(16727907163246744626)
XLA Ops:
  7.3 29.0 %all_gather.3 = f32[4,32,128]{1,0,2:T(4,128)S(1)} all-gather(f32[4,32,16]{1,0,2:T(4,128)S(1)} %copy.69), channel_id=1, replica_groups=mesh['src'=8,'gx'=16,'gy'=4] {'src'}, dimensions={2}, use_global_device_ids=true | all-gather | bytes 73728 | tf_op jit(solution)/shard_map/all_gather | solution.py:104
  36.5 1.3 collective-permute-start.1
  37.8 3.0 collective-permute-start
  40.9 3.9 collective-permute-start.4
  50.0 5.4 collective-permute-start.3
  55.4 2.6 collective-permute-start.2
  58.0 21.9 %collective-permute-done.3 = f32[1,6,1,128]{2,1,3,0:T(8,128)S(1)} collective-permute-done((f32[1,6,1,128]{2,1,3,0:T(8,128)S(1)}, f32[1,6,1,128]{2,1,3,0:T(8,128)S(1)}, u32[]{:S(2)}, u32[]{:S(2)}) %collective-permute-start.3) | collective-permute-done | bytes 3104 | tf_op jit(solution)/shard_map/ppermute | solution.py:23
  80.5 1.7 fusion.293
  82.3 2.3 collective-permute-start.7
  84.7 5.6 collective-permute-start.6
  90.3 2.0 add_divide_fusion
  96.5 3.0 collective-permute-start.8
  100.5 1.9 collective-permute-start.11
  102.4 6.0 %collective-permute-start.10 = (f32[4,6,1,128]{3,2,1,0:T(1,128)S(1)}, f32[4,6,1,128]{3,2,1,0:T(1,128)S(1)}, u32[]{:S(2)}, u32[]{:S(2)}) collective-permute-start(f32[4,6,1,128]{3,2,1,0:T(1,128)S(1)} %get-tuple-element.118), channel_id=1, source_target_pairs={{0,1},{1,2},{2,3},{4,5},{5,6},{6,7},{8,9},{9,10},{10,11},{12,13},{... | collective-permute-start | bytes 36872 | tf_op jit(solution)/shard_map/ppermute | solution.py:20
  108.5 1.4 collective-permute-done.10
  111.4 5.8 collective-permute-start.12
  118.2 1.9 collective-permute-start.15
  120.1 6.0 %collective-permute-start.14 = (f32[4,6,1,128]{3,2,1,0:T(1,128)S(1)}, f32[4,6,1,128]{3,2,1,0:T(1,128)S(1)}, u32[]{:S(2)}, u32[]{:S(2)}) collective-permute-start(f32[4,6,1,128]{3,2,1,0:T(1,128)S(1)} %get-tuple-element.116), channel_id=1, source_target_pairs={{0,1},{1,2},{2,3},{4,5},{5,6},{6,7},{8,9},{9,10},{10,11},{12,13},{... | collective-permute-start | bytes 36872 | tf_op jit(solution)/shard_map/ppermute | solution.py:20
  126.2 1.4 collective-permute-done.14
  127.8 1.4 collective-permute-start.17
  129.3 5.9 collective-permute-start.16
  136.1 1.9 collective-permute-start.19
  138.0 6.0 %collective-permute-start.18 = (f32[4,6,1,128]{3,2,1,0:T(1,128)S(1)}, f32[4,6,1,128]{3,2,1,0:T(1,128)S(1)}, u32[]{:S(2)}, u32[]{:S(2)}) collective-permute-start(f32[4,6,1,128]{3,2,1,0:T(1,128)S(1)} %get-tuple-element.114), channel_id=1, source_target_pairs={{0,1},{1,2},{2,3},{4,5},{5,6},{6,7},{8,9},{9,10},{10,11},{12,13},{... | collective-permute-start | bytes 36872 | tf_op jit(solution)/shard_map/ppermute | solution.py:20
  144.7 5.5 collective-permute-start.32
  153.2 5.8 collective-permute-start.20
  160.5 1.9 collective-permute-start.23
  162.4 6.0 %collective-permute-start.22 = (f32[4,6,1,128]{3,2,1,0:T(1,128)}, f32[4,6,1,128]{3,2,1,0:T(1,128)}, u32[]{:S(2)}, u32[]{:S(2)}) collective-permute-start(f32[4,6,1,128]{3,2,1,0:T(1,128)} %get-tuple-element.112), channel_id=1, source_target_pairs={{0,1},{1,2},{2,3},{4,5},{5,6},{6,7},{8,9},{9,10},{10,11},{12,13},{... | collective-permute-start | bytes 36872 | tf_op jit(solution)/shard_map/ppermute | solution.py:20
  172.6 4.1 collective-permute-start.24
  177.6 1.9 collective-permute-start.27
  179.5 6.0 %collective-permute-start.26 = (f32[4,6,1,128]{3,2,1,0:T(1,128)S(1)}, f32[4,6,1,128]{3,2,1,0:T(1,128)S(1)}, u32[]{:S(2)}, u32[]{:S(2)}) collective-permute-start(f32[4,6,1,128]{3,2,1,0:T(1,128)S(1)} %get-tuple-element.110), channel_id=1, source_target_pairs={{0,1},{1,2},{2,3},{4,5},{5,6},{6,7},{8,9},{9,10},{10,11},{12,13},{... | collective-permute-start | bytes 36872 | tf_op jit(solution)/shard_map/ppermute | solution.py:20
  185.6 1.3 collective-permute-done.26
  188.6 5.2 collective-permute-start.28
  194.7 1.9 collective-permute-start.31
  196.6 6.0 %collective-permute-start.30 = (f32[4,6,1,128]{3,2,1,0:T(1,128)S(1)}, f32[4,6,1,128]{3,2,1,0:T(1,128)S(1)}, u32[]{:S(2)}, u32[]{:S(2)}) collective-permute-start(f32[4,6,1,128]{3,2,1,0:T(1,128)S(1)} %get-tuple-element.108), channel_id=1, source_target_pairs={{0,1},{1,2},{2,3},{4,5},{5,6},{6,7},{8,9},{9,10},{10,11},{12,13},{... | collective-permute-start | bytes 36872 | tf_op jit(solution)/shard_map/ppermute | solution.py:20
  202.7 1.9 collective-permute-start.35
  204.6 6.0 %collective-permute-start.34 = (f32[4,6,1,128]{3,2,1,0:T(1,128)S(1)}, f32[4,6,1,128]{3,2,1,0:T(1,128)S(1)}, u32[]{:S(2)}, u32[]{:S(2)}) collective-permute-start(f32[4,6,1,128]{3,2,1,0:T(1,128)S(1)} %get-tuple-element.106), channel_id=1, source_target_pairs={{0,1},{1,2},{2,3},{4,5},{5,6},{6,7},{8,9},{9,10},{10,11},{12,13},{... | collective-permute-start | bytes 36872 | tf_op jit(solution)/shard_map/ppermute | solution.py:20
  212.4 144.6 %psum.14 = f32[4,128]{1,0:T(4,128)S(1)} all-reduce(f32[4,128]{1,0:T(4,128)S(1)} %fusion.300), channel_id=1, replica_groups=mesh['src'=8,'gx'=16,'gy'=4] {'gx','gy'}, use_global_device_ids=true, to_apply=%region_0.1 | all-reduce | flops 512 | bytes 4096 | tf_op jit(solution)/shard_map/psum | solution.py:140
  359.9 3.0 collective-permute-start.36
  363.9 4.6 collective-permute-start.39
  368.5 3.3 collective-permute-start.38
  371.9 3.1 collective-permute-done.38
  376.6 3.0 collective-permute-start.40
  380.6 1.9 collective-permute-start.43
  382.5 6.0 %collective-permute-start.42 = (f32[4,6,1,128]{3,2,1,0:T(1,128)S(1)}, f32[4,6,1,128]{3,2,1,0:T(1,128)S(1)}, u32[]{:S(2)}, u32[]{:S(2)}) collective-permute-start(f32[4,6,1,128]{3,2,1,0:T(1,128)S(1)} %get-tuple-element.102), channel_id=1, source_target_pairs={{0,1},{1,2},{2,3},{4,5},{5,6},{6,7},{8,9},{9,10},{10,11},{12,13},{... | collective-permute-start | bytes 36872 | tf_op jit(solution)/shard_map/ppermute | solution.py:20
  388.5 1.4 collective-permute-done.42
  391.5 4.1 collective-permute-start.44
  396.6 1.9 collective-permute-start.47
  398.5 6.2 %collective-permute-start.46 = (f32[4,6,1,128]{3,2,1,0:T(1,128)S(1)}, f32[4,6,1,128]{3,2,1,0:T(1,128)S(1)}, u32[]{:S(2)}, u32[]{:S(2)}) collective-permute-start(f32[4,6,1,128]{3,2,1,0:T(1,128)S(1)} %get-tuple-element.100), channel_id=1, source_target_pairs={{0,1},{1,2},{2,3},{4,5},{5,6},{6,7},{8,9},{9,10},{10,11},{12,13},{... | collective-permute-start | bytes 36872 | tf_op jit(solution)/shard_map/ppermute | solution.py:20
  407.5 5.9 collective-permute-start.48
  414.3 1.9 collective-permute-start.51
  416.3 6.0 %collective-permute-start.50 = (f32[4,6,1,128]{3,2,1,0:T(1,128)S(1)}, f32[4,6,1,128]{3,2,1,0:T(1,128)S(1)}, u32[]{:S(2)}, u32[]{:S(2)}) collective-permute-start(f32[4,6,1,128]{3,2,1,0:T(1,128)S(1)} %get-tuple-element.98), channel_id=1, source_target_pairs={{0,1},{1,2},{2,3},{4,5},{5,6},{6,7},{8,9},{9,10},{10,11},{12,13},{... | collective-permute-start | bytes 36872 | tf_op jit(solution)/shard_map/ppermute | solution.py:20
  422.3 1.4 collective-permute-done.50
  425.3 5.6 collective-permute-start.52
  431.8 1.9 collective-permute-start.55
  433.7 6.0 %collective-permute-start.54 = (f32[4,6,1,128]{3,2,1,0:T(1,128)S(1)}, f32[4,6,1,128]{3,2,1,0:T(1,128)S(1)}, u32[]{:S(2)}, u32[]{:S(2)}) collective-permute-start(f32[4,6,1,128]{3,2,1,0:T(1,128)S(1)} %get-tuple-element.96), channel_id=1, source_target_pairs={{0,1},{1,2},{2,3},{4,5},{5,6},{6,7},{8,9},{9,10},{10,11},{12,13},{... | collective-permute-start | bytes 36872 | tf_op jit(solution)/shard_map/ppermute | solution.py:20
  439.8 1.4 collective-permute-done.54
  442.8 5.6 collective-permute-start.56
  449.3 1.9 collective-permute-start.59
  451.2 6.0 %collective-permute-start.58 = (f32[4,6,1,128]{3,2,1,0:T(1,128)S(1)}, f32[4,6,1,128]{3,2,1,0:T(1,128)S(1)}, u32[]{:S(2)}, u32[]{:S(2)}) collective-permute-start(f32[4,6,1,128]{3,2,1,0:T(1,128)S(1)} %get-tuple-element.94), channel_id=1, source_target_pairs={{0,1},{1,2},{2,3},{4,5},{5,6},{6,7},{8,9},{9,10},{10,11},{12,13},{... | collective-permute-start | bytes 36872 | tf_op jit(solution)/shard_map/ppermute | solution.py:20
  457.3 1.4 collective-permute-done.58
  460.4 5.7 collective-permute-start.60
  467.2 2.1 collective-permute-start.63
  469.2 6.0 %collective-permute-start.62 = (f32[8,6,1,128]{3,2,1,0:T(1,128)S(1)}, f32[8,6,1,128]{3,2,1,0:T(1,128)S(1)}, u32[]{:S(2)}, u32[]{:S(2)}) collective-permute-start(f32[8,6,1,128]{3,2,1,0:T(1,128)S(1)} %get-tuple-element.82), channel_id=1, source_target_pairs={{0,1},{1,2},{2,3},{4,5},{5,6},{6,7},{8,9},{9,10},{10,11},{12,13},{... | collective-permute-start | bytes 73736 | tf_op jit(solution)/shard_map/ppermute | solution.py:20
  477.8 106.1 %all-reduce.21.cloned.1.call-done = f32[4,32,128]{2,1,0:T(8,128)} async-done(((f32[4,32,128]{2,1,0:T(8,128)}), f32[4,32,128]{2,1,0:T(8,128)}) %all-reduce.21.cloned.1.call-update) | async-done | bytes 65552 | tf_op jit(solution)/shard_map/psum | solution.py:99
  (203 shorter events, 54.0 us)
Async XLA Ops:
  6.5 577.4 %all-reduce.21.cloned.1.call-start = ((), (), s32[]{:S(2)}) async-start(), calls=%async_computation | async-start | bytes 131072 | tf_op jit(solution)/shard_map/psum | solution.py:99
  36.5 13.1 %collective-permute-start.1 = (f32[1,1,32,128]{2,1,3,0:T(1,128)S(1)}, f32[1,1,32,128]{2,1,3,0:T(1,128)S(1)}, u32[]{:S(2)}, u32[]{:S(2)}) collective-permute-start(f32[1,1,32,128]{2,1,3,0:T(1,128)S(1)} %get-tuple-element.153), channel_id=1, source_target_pairs={{4,0},{8,4},{12,8},{16,12},{20,16},{24,20},{28,24},{32,28},{36,32}... | collective-permute-start | bytes 49160 | tf_op jit(solution)/shard_map/ppermute | solution.py:23
  37.8 11.8 %collective-permute-start = (f32[1,1,32,128]{2,1,3,0:T(1,128)S(1)}, f32[1,1,32,128]{2,1,3,0:T(1,128)S(1)}, u32[]{:S(2)}, u32[]{:S(2)}) collective-permute-start(f32[1,1,32,128]{2,1,3,0:T(1,128)S(1)} %get-tuple-element.152), channel_id=1, source_target_pairs={{0,4},{4,8},{8,12},{12,16},{16,20},{20,24},{24,28},{28,32},{32,36}... | collective-permute-start | bytes 49160 | tf_op jit(solution)/shard_map/ppermute | solution.py:20
  40.9 41.4 %collective-permute-start.4 = (f32[4,1,32,128]{3,2,1,0:T(8,128)S(1)}, f32[4,1,32,128]{3,2,1,0:T(8,128)S(1)}, u32[]{:S(2)}, u32[]{:S(2)}) collective-permute-start(f32[4,1,32,128]{3,2,1,0:T(8,128)S(1)} %get-tuple-element.151), channel_id=1, source_target_pairs={{0,4},{4,8},{8,12},{12,16},{16,20},{20,24},{24,28},{28,32},{32,36}... | collective-permute-start | bytes 196616 | tf_op jit(solution)/shard_map/ppermute | solution.py:20
  44.8 37.5 %collective-permute-start.5 = (f32[4,1,32,128]{3,2,1,0:T(8,128)S(1)}, f32[4,1,32,128]{3,2,1,0:T(8,128)S(1)}, u32[]{:S(2)}, u32[]{:S(2)}) collective-permute-start(f32[4,1,32,128]{3,2,1,0:T(8,128)S(1)} %get-tuple-element.150), channel_id=1, source_target_pairs={{4,0},{8,4},{12,8},{16,12},{20,16},{24,20},{28,24},{32,28},{36,32}... | collective-permute-start | bytes 196616 | tf_op jit(solution)/shard_map/ppermute | solution.py:23
  50.0 29.9 %collective-permute-start.3 = (f32[1,6,1,128]{2,1,3,0:T(8,128)S(1)}, f32[1,6,1,128]{2,1,3,0:T(8,128)S(1)}, u32[]{:S(2)}, u32[]{:S(2)}) collective-permute-start(f32[1,6,1,128]{2,1,3,0:T(8,128)S(1)} %get-tuple-element.93), channel_id=1, source_target_pairs={{1,0},{2,1},{3,2},{5,4},{6,5},{7,6},{9,8},{10,9},{11,10},{13,12},{... | collective-permute-start | bytes 9224 | tf_op jit(solution)/shard_map/ppermute | solution.py:23
  55.4 24.5 %collective-permute-start.2 = (f32[1,6,1,128]{2,1,3,0:T(8,128)S(1)}, f32[1,6,1,128]{2,1,3,0:T(8,128)S(1)}, u32[]{:S(2)}, u32[]{:S(2)}) collective-permute-start(f32[1,6,1,128]{2,1,3,0:T(8,128)S(1)} %get-tuple-element.92), channel_id=1, source_target_pairs={{0,1},{1,2},{2,3},{4,5},{5,6},{6,7},{8,9},{9,10},{10,11},{12,13},{... | collective-permute-start | bytes 9224 | tf_op jit(solution)/shard_map/ppermute | solution.py:20
  82.3 11.8 %collective-permute-start.7 = (f32[4,6,1,128]{3,2,1,0:T(1,128)S(1)}, f32[4,6,1,128]{3,2,1,0:T(1,128)S(1)}, u32[]{:S(2)}, u32[]{:S(2)}) collective-permute-start(f32[4,6,1,128]{3,2,1,0:T(1,128)S(1)} %get-tuple-element.121), channel_id=1, source_target_pairs={{1,0},{2,1},{3,2},{5,4},{6,5},{7,6},{9,8},{10,9},{11,10},{13,12},{... | collective-permute-start | bytes 36872 | tf_op jit(solution)/shard_map/ppermute | solution.py:23
  84.7 9.4 %collective-permute-start.6 = (f32[4,6,1,128]{3,2,1,0:T(1,128)S(1)}, f32[4,6,1,128]{3,2,1,0:T(1,128)S(1)}, u32[]{:S(2)}, u32[]{:S(2)}) collective-permute-start(f32[4,6,1,128]{3,2,1,0:T(1,128)S(1)} %get-tuple-element.120), channel_id=1, source_target_pairs={{0,1},{1,2},{2,3},{4,5},{5,6},{6,7},{8,9},{9,10},{10,11},{12,13},{... | collective-permute-start | bytes 36872 | tf_op jit(solution)/shard_map/ppermute | solution.py:20
  95.2 4.3 collective-permute-start.9
  96.5 3.9 collective-permute-start.8
  100.5 8.0 %collective-permute-start.11 = (f32[4,6,1,128]{3,2,1,0:T(1,128)S(1)}, f32[4,6,1,128]{3,2,1,0:T(1,128)S(1)}, u32[]{:S(2)}, u32[]{:S(2)}) collective-permute-start(f32[4,6,1,128]{3,2,1,0:T(1,128)S(1)} %get-tuple-element.119), channel_id=1, source_target_pairs={{1,0},{2,1},{3,2},{5,4},{6,5},{7,6},{9,8},{10,9},{11,10},{13,12},{... | collective-permute-start | bytes 36872 | tf_op jit(solution)/shard_map/ppermute | solution.py:23
  102.4 7.4 %collective-permute-start.10 = (f32[4,6,1,128]{3,2,1,0:T(1,128)S(1)}, f32[4,6,1,128]{3,2,1,0:T(1,128)S(1)}, u32[]{:S(2)}, u32[]{:S(2)}) collective-permute-start(f32[4,6,1,128]{3,2,1,0:T(1,128)S(1)} %get-tuple-element.118), channel_id=1, source_target_pairs={{0,1},{1,2},{2,3},{4,5},{5,6},{6,7},{8,9},{9,10},{10,11},{12,13},{... | collective-permute-start | bytes 36872 | tf_op jit(solution)/shard_map/ppermute | solution.py:20
  110.1 7.1 %collective-permute-start.13 = (f32[4,1,32,128]{3,2,1,0:T(8,128)S(1)}, f32[4,1,32,128]{3,2,1,0:T(8,128)S(1)}, u32[]{:S(2)}, u32[]{:S(2)}) collective-permute-start(f32[4,1,32,128]{3,2,1,0:T(8,128)S(1)} %get-tuple-element.147), channel_id=1, source_target_pairs={{4,0},{8,4},{12,8},{16,12},{20,16},{24,20},{28,24},{32,28},{36,32}... | collective-permute-start | bytes 196616 | tf_op jit(solution)/shard_map/ppermute | solution.py:23
  111.4 6.7 %collective-permute-start.12 = (f32[4,1,32,128]{3,2,1,0:T(8,128)S(1)}, f32[4,1,32,128]{3,2,1,0:T(8,128)S(1)}, u32[]{:S(2)}, u32[]{:S(2)}) collective-permute-start(f32[4,1,32,128]{3,2,1,0:T(8,128)S(1)} %get-tuple-element.146), channel_id=1, source_target_pairs={{0,4},{4,8},{8,12},{12,16},{16,20},{20,24},{24,28},{28,32},{32,36}... | collective-permute-start | bytes 196616 | tf_op jit(solution)/shard_map/ppermute | solution.py:20
  118.2 8.0 %collective-permute-start.15 = (f32[4,6,1,128]{3,2,1,0:T(1,128)S(1)}, f32[4,6,1,128]{3,2,1,0:T(1,128)S(1)}, u32[]{:S(2)}, u32[]{:S(2)}) collective-permute-start(f32[4,6,1,128]{3,2,1,0:T(1,128)S(1)} %get-tuple-element.117), channel_id=1, source_target_pairs={{1,0},{2,1},{3,2},{5,4},{6,5},{7,6},{9,8},{10,9},{11,10},{13,12},{... | collective-permute-start | bytes 36872 | tf_op jit(solution)/shard_map/ppermute | solution.py:23
  120.1 7.4 %collective-permute-start.14 = (f32[4,6,1,128]{3,2,1,0:T(1,128)S(1)}, f32[4,6,1,128]{3,2,1,0:T(1,128)S(1)}, u32[]{:S(2)}, u32[]{:S(2)}) collective-permute-start(f32[4,6,1,128]{3,2,1,0:T(1,128)S(1)} %get-tuple-element.116), channel_id=1, source_target_pairs={{0,1},{1,2},{2,3},{4,5},{5,6},{6,7},{8,9},{9,10},{10,11},{12,13},{... | collective-permute-start | bytes 36872 | tf_op jit(solution)/shard_map/ppermute | solution.py:20
  127.8 7.3 %collective-permute-start.17 = (f32[4,1,32,128]{3,2,1,0:T(8,128)S(1)}, f32[4,1,32,128]{3,2,1,0:T(8,128)S(1)}, u32[]{:S(2)}, u32[]{:S(2)}) collective-permute-start(f32[4,1,32,128]{3,2,1,0:T(8,128)S(1)} %get-tuple-element.145), channel_id=1, source_target_pairs={{4,0},{8,4},{12,8},{16,12},{20,16},{24,20},{28,24},{32,28},{36,32}... | collective-permute-start | bytes 196616 | tf_op jit(solution)/shard_map/ppermute | solution.py:23
  129.3 6.8 %collective-permute-start.16 = (f32[4,1,32,128]{3,2,1,0:T(8,128)S(1)}, f32[4,1,32,128]{3,2,1,0:T(8,128)S(1)}, u32[]{:S(2)}, u32[]{:S(2)}) collective-permute-start(f32[4,1,32,128]{3,2,1,0:T(8,128)S(1)} %get-tuple-element.144), channel_id=1, source_target_pairs={{0,4},{4,8},{8,12},{12,16},{16,20},{20,24},{24,28},{28,32},{32,36}... | collective-permute-start | bytes 196616 | tf_op jit(solution)/shard_map/ppermute | solution.py:20
  136.1 15.5 %collective-permute-start.19 = (f32[4,6,1,128]{3,2,1,0:T(1,128)S(1)}, f32[4,6,1,128]{3,2,1,0:T(1,128)S(1)}, u32[]{:S(2)}, u32[]{:S(2)}) collective-permute-start(f32[4,6,1,128]{3,2,1,0:T(1,128)S(1)} %get-tuple-element.115), channel_id=1, source_target_pairs={{1,0},{2,1},{3,2},{5,4},{6,5},{7,6},{9,8},{10,9},{11,10},{13,12},{... | collective-permute-start | bytes 36872 | tf_op jit(solution)/shard_map/ppermute | solution.py:23
  138.0 13.6 %collective-permute-start.18 = (f32[4,6,1,128]{3,2,1,0:T(1,128)S(1)}, f32[4,6,1,128]{3,2,1,0:T(1,128)S(1)}, u32[]{:S(2)}, u32[]{:S(2)}) collective-permute-start(f32[4,6,1,128]{3,2,1,0:T(1,128)S(1)} %get-tuple-element.114), channel_id=1, source_target_pairs={{0,1},{1,2},{2,3},{4,5},{5,6},{6,7},{8,9},{9,10},{10,11},{12,13},{... | collective-permute-start | bytes 36872 | tf_op jit(solution)/shard_map/ppermute | solution.py:20
  144.7 32.0 %collective-permute-start.32 = (f32[4,1,32,128]{3,2,1,0:T(8,128)}, f32[4,1,32,128]{3,2,1,0:T(8,128)S(1)}, u32[]{:S(2)}, u32[]{:S(2)}) collective-permute-start(f32[4,1,32,128]{3,2,1,0:T(8,128)} %get-tuple-element.137), channel_id=1, source_target_pairs={{0,4},{4,8},{8,12},{12,16},{16,20},{20,24},{24,28},{28,32},{32,36}... | collective-permute-start | bytes 196616 | tf_op jit(solution)/shard_map/ppermute | solution.py:20
  150.2 43.6 %collective-permute-start.33 = (f32[4,1,32,128]{3,2,1,0:T(8,128)}, f32[4,1,32,128]{3,2,1,0:T(8,128)}, u32[]{:S(2)}, u32[]{:S(2)}) collective-permute-start(f32[4,1,32,128]{3,2,1,0:T(8,128)} %get-tuple-element.136), channel_id=1, source_target_pairs={{4,0},{8,4},{12,8},{16,12},{20,16},{24,20},{28,24},{32,28},{36,32}... | collective-permute-start | bytes 196616 | tf_op jit(solution)/shard_map/ppermute | solution.py:23
  151.9 7.7 %collective-permute-start.21 = (f32[4,1,32,128]{3,2,1,0:T(8,128)S(1)}, f32[4,1,32,128]{3,2,1,0:T(8,128)S(1)}, u32[]{:S(2)}, u32[]{:S(2)}) collective-permute-start(f32[4,1,32,128]{3,2,1,0:T(8,128)S(1)} %get-tuple-element.143), channel_id=1, source_target_pairs={{4,0},{8,4},{12,8},{16,12},{20,16},{24,20},{28,24},{32,28},{36,32}... | collective-permute-start | bytes 196616 | tf_op jit(solution)/shard_map/ppermute | solution.py:23
  153.2 6.7 %collective-permute-start.20 = (f32[4,1,32,128]{3,2,1,0:T(8,128)S(1)}, f32[4,1,32,128]{3,2,1,0:T(8,128)S(1)}, u32[]{:S(2)}, u32[]{:S(2)}) collective-permute-start(f32[4,1,32,128]{3,2,1,0:T(8,128)S(1)} %get-tuple-element.142), channel_id=1, source_target_pairs={{0,4},{4,8},{8,12},{12,16},{16,20},{20,24},{24,28},{28,32},{32,36}... | collective-permute-start | bytes 196616 | tf_op jit(solution)/shard_map/ppermute | solution.py:20
  160.5 9.8 %collective-permute-start.23 = (f32[4,6,1,128]{3,2,1,0:T(1,128)}, f32[4,6,1,128]{3,2,1,0:T(1,128)}, u32[]{:S(2)}, u32[]{:S(2)}) collective-permute-start(f32[4,6,1,128]{3,2,1,0:T(1,128)} %get-tuple-element.113), channel_id=1, source_target_pairs={{1,0},{2,1},{3,2},{5,4},{6,5},{7,6},{9,8},{10,9},{11,10},{13,12},{... | collective-permute-start | bytes 36872 | tf_op jit(solution)/shard_map/ppermute | solution.py:23
  162.4 7.8 %collective-permute-start.22 = (f32[4,6,1,128]{3,2,1,0:T(1,128)}, f32[4,6,1,128]{3,2,1,0:T(1,128)}, u32[]{:S(2)}, u32[]{:S(2)}) collective-permute-start(f32[4,6,1,128]{3,2,1,0:T(1,128)} %get-tuple-element.112), channel_id=1, source_target_pairs={{0,1},{1,2},{2,3},{4,5},{5,6},{6,7},{8,9},{9,10},{10,11},{12,13},{... | collective-permute-start | bytes 36872 | tf_op jit(solution)/shard_map/ppermute | solution.py:20
  171.3 5.5 collective-permute-start.25
  172.6 5.0 collective-permute-start.24
  177.6 8.0 %collective-permute-start.27 = (f32[4,6,1,128]{3,2,1,0:T(1,128)S(1)}, f32[4,6,1,128]{3,2,1,0:T(1,128)S(1)}, u32[]{:S(2)}, u32[]{:S(2)}) collective-permute-start(f32[4,6,1,128]{3,2,1,0:T(1,128)S(1)} %get-tuple-element.111), channel_id=1, source_target_pairs={{1,0},{2,1},{3,2},{5,4},{6,5},{7,6},{9,8},{10,9},{11,10},{13,12},{... | collective-permute-start | bytes 36872 | tf_op jit(solution)/shard_map/ppermute | solution.py:23
  179.5 7.4 %collective-permute-start.26 = (f32[4,6,1,128]{3,2,1,0:T(1,128)S(1)}, f32[4,6,1,128]{3,2,1,0:T(1,128)S(1)}, u32[]{:S(2)}, u32[]{:S(2)}) collective-permute-start(f32[4,6,1,128]{3,2,1,0:T(1,128)S(1)} %get-tuple-element.110), channel_id=1, source_target_pairs={{0,1},{1,2},{2,3},{4,5},{5,6},{6,7},{8,9},{9,10},{10,11},{12,13},{... | collective-permute-start | bytes 36872 | tf_op jit(solution)/shard_map/ppermute | solution.py:20
  187.3 7.4 %collective-permute-start.29 = (f32[4,1,32,128]{3,2,1,0:T(8,128)S(1)}, f32[4,1,32,128]{3,2,1,0:T(8,128)S(1)}, u32[]{:S(2)}, u32[]{:S(2)}) collective-permute-start(f32[4,1,32,128]{3,2,1,0:T(8,128)S(1)} %get-tuple-element.139), channel_id=1, source_target_pairs={{4,0},{8,4},{12,8},{16,12},{20,16},{24,20},{28,24},{32,28},{36,32}... | collective-permute-start | bytes 196616 | tf_op jit(solution)/shard_map/ppermute | solution.py:23
  188.6 6.1 %collective-permute-start.28 = (f32[4,1,32,128]{3,2,1,0:T(8,128)S(1)}, f32[4,1,32,128]{3,2,1,0:T(8,128)S(1)}, u32[]{:S(2)}, u32[]{:S(2)}) collective-permute-start(f32[4,1,32,128]{3,2,1,0:T(8,128)S(1)} %get-tuple-element.138), channel_id=1, source_target_pairs={{0,4},{4,8},{8,12},{12,16},{16,20},{20,24},{24,28},{28,32},{32,36}... | collective-permute-start | bytes 196616 | tf_op jit(solution)/shard_map/ppermute | solution.py:20
  194.7 16.0 %collective-permute-start.31 = (f32[4,6,1,128]{3,2,1,0:T(1,128)S(1)}, f32[4,6,1,128]{3,2,1,0:T(1,128)S(1)}, u32[]{:S(2)}, u32[]{:S(2)}) collective-permute-start(f32[4,6,1,128]{3,2,1,0:T(1,128)S(1)} %get-tuple-element.109), channel_id=1, source_target_pairs={{1,0},{2,1},{3,2},{5,4},{6,5},{7,6},{9,8},{10,9},{11,10},{13,12},{... | collective-permute-start | bytes 36872 | tf_op jit(solution)/shard_map/ppermute | solution.py:23
  196.6 14.0 %collective-permute-start.30 = (f32[4,6,1,128]{3,2,1,0:T(1,128)S(1)}, f32[4,6,1,128]{3,2,1,0:T(1,128)S(1)}, u32[]{:S(2)}, u32[]{:S(2)}) collective-permute-start(f32[4,6,1,128]{3,2,1,0:T(1,128)S(1)} %get-tuple-element.108), channel_id=1, source_target_pairs={{0,1},{1,2},{2,3},{4,5},{5,6},{6,7},{8,9},{9,10},{10,11},{12,13},{... | collective-permute-start | bytes 36872 | tf_op jit(solution)/shard_map/ppermute | solution.py:20
  202.7 154.8 %collective-permute-start.35 = (f32[4,6,1,128]{3,2,1,0:T(1,128)S(1)}, f32[4,6,1,128]{3,2,1,0:T(1,128)S(1)}, u32[]{:S(2)}, u32[]{:S(2)}) collective-permute-start(f32[4,6,1,128]{3,2,1,0:T(1,128)S(1)} %get-tuple-element.107), channel_id=1, source_target_pairs={{1,0},{2,1},{3,2},{5,4},{6,5},{7,6},{9,8},{10,9},{11,10},{13,12},{... | collective-permute-start | bytes 36872 | tf_op jit(solution)/shard_map/ppermute | solution.py:23
  204.6 152.9 %collective-permute-start.34 = (f32[4,6,1,128]{3,2,1,0:T(1,128)S(1)}, f32[4,6,1,128]{3,2,1,0:T(1,128)S(1)}, u32[]{:S(2)}, u32[]{:S(2)}) collective-permute-start(f32[4,6,1,128]{3,2,1,0:T(1,128)S(1)} %get-tuple-element.106), channel_id=1, source_target_pairs={{0,1},{1,2},{2,3},{4,5},{5,6},{6,7},{8,9},{9,10},{10,11},{12,13},{... | collective-permute-start | bytes 36872 | tf_op jit(solution)/shard_map/ppermute | solution.py:20
  358.6 4.3 collective-permute-start.37
  359.9 3.9 collective-permute-start.36
  363.9 8.0 %collective-permute-start.39 = (f32[4,6,1,128]{3,2,1,0:T(1,128)S(1)}, f32[4,6,1,128]{3,2,1,0:T(1,128)S(1)}, u32[]{:S(2)}, u32[]{:S(2)}) collective-permute-start(f32[4,6,1,128]{3,2,1,0:T(1,128)S(1)} %get-tuple-element.105), channel_id=1, source_target_pairs={{1,0},{2,1},{3,2},{5,4},{6,5},{7,6},{9,8},{10,9},{11,10},{13,12},{... | collective-permute-start | bytes 36872 | tf_op jit(solution)/shard_map/ppermute | solution.py:23
  368.5 6.5 %collective-permute-start.38 = (f32[4,6,1,128]{3,2,1,0:T(1,128)S(1)}, f32[4,6,1,128]{3,2,1,0:T(1,128)S(1)}, u32[]{:S(2)}, u32[]{:S(2)}) collective-permute-start(f32[4,6,1,128]{3,2,1,0:T(1,128)S(1)} %get-tuple-element.104), channel_id=1, source_target_pairs={{0,1},{1,2},{2,3},{4,5},{5,6},{6,7},{8,9},{9,10},{10,11},{12,13},{... | collective-permute-start | bytes 36872 | tf_op jit(solution)/shard_map/ppermute | solution.py:20
  375.3 4.3 collective-permute-start.41
  380.6 8.0 %collective-permute-start.43 = (f32[4,6,1,128]{3,2,1,0:T(1,128)S(1)}, f32[4,6,1,128]{3,2,1,0:T(1,128)S(1)}, u32[]{:S(2)}, u32[]{:S(2)}) collective-permute-start(f32[4,6,1,128]{3,2,1,0:T(1,128)S(1)} %get-tuple-element.103), channel_id=1, source_target_pairs={{1,0},{2,1},{3,2},{5,4},{6,5},{7,6},{9,8},{10,9},{11,10},{13,12},{... | collective-permute-start | bytes 36872 | tf_op jit(solution)/shard_map/ppermute | solution.py:23
  382.5 7.4 %collective-permute-start.42 = (f32[4,6,1,128]{3,2,1,0:T(1,128)S(1)}, f32[4,6,1,128]{3,2,1,0:T(1,128)S(1)}, u32[]{:S(2)}, u32[]{:S(2)}) collective-permute-start(f32[4,6,1,128]{3,2,1,0:T(1,128)S(1)} %get-tuple-element.102), channel_id=1, source_target_pairs={{0,1},{1,2},{2,3},{4,5},{5,6},{6,7},{8,9},{9,10},{10,11},{12,13},{... | collective-permute-start | bytes 36872 | tf_op jit(solution)/shard_map/ppermute | solution.py:20
  390.2 5.4 collective-permute-start.45
  391.5 5.0 collective-permute-start.44
  396.6 8.2 %collective-permute-start.47 = (f32[4,6,1,128]{3,2,1,0:T(1,128)S(1)}, f32[4,6,1,128]{3,2,1,0:T(1,128)S(1)}, u32[]{:S(2)}, u32[]{:S(2)}) collective-permute-start(f32[4,6,1,128]{3,2,1,0:T(1,128)S(1)} %get-tuple-element.101), channel_id=1, source_target_pairs={{1,0},{2,1},{3,2},{5,4},{6,5},{7,6},{9,8},{10,9},{11,10},{13,12},{... | collective-permute-start | bytes 36872 | tf_op jit(solution)/shard_map/ppermute | solution.py:23
  398.5 7.4 %collective-permute-start.46 = (f32[4,6,1,128]{3,2,1,0:T(1,128)S(1)}, f32[4,6,1,128]{3,2,1,0:T(1,128)S(1)}, u32[]{:S(2)}, u32[]{:S(2)}) collective-permute-start(f32[4,6,1,128]{3,2,1,0:T(1,128)S(1)} %get-tuple-element.100), channel_id=1, source_target_pairs={{0,1},{1,2},{2,3},{4,5},{5,6},{6,7},{8,9},{9,10},{10,11},{12,13},{... | collective-permute-start | bytes 36872 | tf_op jit(solution)/shard_map/ppermute | solution.py:20
  406.2 7.2 %collective-permute-start.49 = (f32[4,1,32,128]{3,2,1,0:T(8,128)S(1)}, f32[4,1,32,128]{3,2,1,0:T(8,128)S(1)}, u32[]{:S(2)}, u32[]{:S(2)}) collective-permute-start(f32[4,1,32,128]{3,2,1,0:T(8,128)S(1)} %get-tuple-element.129), channel_id=1, source_target_pairs={{4,0},{8,4},{12,8},{16,12},{20,16},{24,20},{28,24},{32,28},{36,32}... | collective-permute-start | bytes 196616 | tf_op jit(solution)/shard_map/ppermute | solution.py:23
  407.5 6.8 %collective-permute-start.48 = (f32[4,1,32,128]{3,2,1,0:T(8,128)S(1)}, f32[4,1,32,128]{3,2,1,0:T(8,128)S(1)}, u32[]{:S(2)}, u32[]{:S(2)}) collective-permute-start(f32[4,1,32,128]{3,2,1,0:T(8,128)S(1)} %get-tuple-element.128), channel_id=1, source_target_pairs={{0,4},{4,8},{8,12},{12,16},{16,20},{20,24},{24,28},{28,32},{32,36}... | collective-permute-start | bytes 196616 | tf_op jit(solution)/shard_map/ppermute | solution.py:20
  414.3 8.0 %collective-permute-start.51 = (f32[4,6,1,128]{3,2,1,0:T(1,128)S(1)}, f32[4,6,1,128]{3,2,1,0:T(1,128)S(1)}, u32[]{:S(2)}, u32[]{:S(2)}) collective-permute-start(f32[4,6,1,128]{3,2,1,0:T(1,128)S(1)} %get-tuple-element.99), channel_id=1, source_target_pairs={{1,0},{2,1},{3,2},{5,4},{6,5},{7,6},{9,8},{10,9},{11,10},{13,12},{... | collective-permute-start | bytes 36872 | tf_op jit(solution)/shard_map/ppermute | solution.py:23
  416.3 7.4 %collective-permute-start.50 = (f32[4,6,1,128]{3,2,1,0:T(1,128)S(1)}, f32[4,6,1,128]{3,2,1,0:T(1,128)S(1)}, u32[]{:S(2)}, u32[]{:S(2)}) collective-permute-start(f32[4,6,1,128]{3,2,1,0:T(1,128)S(1)} %get-tuple-element.98), channel_id=1, source_target_pairs={{0,1},{1,2},{2,3},{4,5},{5,6},{6,7},{8,9},{9,10},{10,11},{12,13},{... | collective-permute-start | bytes 36872 | tf_op jit(solution)/shard_map/ppermute | solution.py:20
  424.0 6.9 %collective-permute-start.53 = (f32[4,1,32,128]{3,2,1,0:T(8,128)S(1)}, f32[4,1,32,128]{3,2,1,0:T(8,128)S(1)}, u32[]{:S(2)}, u32[]{:S(2)}) collective-permute-start(f32[4,1,32,128]{3,2,1,0:T(8,128)S(1)} %get-tuple-element.127), channel_id=1, source_target_pairs={{4,0},{8,4},{12,8},{16,12},{20,16},{24,20},{28,24},{32,28},{36,32}... | collective-permute-start | bytes 196616 | tf_op jit(solution)/shard_map/ppermute | solution.py:23
  425.3 6.5 %collective-permute-start.52 = (f32[4,1,32,128]{3,2,1,0:T(8,128)S(1)}, f32[4,1,32,128]{3,2,1,0:T(8,128)S(1)}, u32[]{:S(2)}, u32[]{:S(2)}) collective-permute-start(f32[4,1,32,128]{3,2,1,0:T(8,128)S(1)} %get-tuple-element.126), channel_id=1, source_target_pairs={{0,4},{4,8},{8,12},{12,16},{16,20},{20,24},{24,28},{28,32},{32,36}... | collective-permute-start | bytes 196616 | tf_op jit(solution)/shard_map/ppermute | solution.py:20
  431.8 8.0 %collective-permute-start.55 = (f32[4,6,1,128]{3,2,1,0:T(1,128)S(1)}, f32[4,6,1,128]{3,2,1,0:T(1,128)S(1)}, u32[]{:S(2)}, u32[]{:S(2)}) collective-permute-start(f32[4,6,1,128]{3,2,1,0:T(1,128)S(1)} %get-tuple-element.97), channel_id=1, source_target_pairs={{1,0},{2,1},{3,2},{5,4},{6,5},{7,6},{9,8},{10,9},{11,10},{13,12},{... | collective-permute-start | bytes 36872 | tf_op jit(solution)/shard_map/ppermute | solution.py:23
  433.7 7.4 %collective-permute-start.54 = (f32[4,6,1,128]{3,2,1,0:T(1,128)S(1)}, f32[4,6,1,128]{3,2,1,0:T(1,128)S(1)}, u32[]{:S(2)}, u32[]{:S(2)}) collective-permute-start(f32[4,6,1,128]{3,2,1,0:T(1,128)S(1)} %get-tuple-element.96), channel_id=1, source_target_pairs={{0,1},{1,2},{2,3},{4,5},{5,6},{6,7},{8,9},{9,10},{10,11},{12,13},{... | collective-permute-start | bytes 36872 | tf_op jit(solution)/shard_map/ppermute | solution.py:20
  441.5 6.9 %collective-permute-start.57 = (f32[4,1,32,128]{3,2,1,0:T(8,128)S(1)}, f32[4,1,32,128]{3,2,1,0:T(8,128)S(1)}, u32[]{:S(2)}, u32[]{:S(2)}) collective-permute-start(f32[4,1,32,128]{3,2,1,0:T(8,128)S(1)} %get-tuple-element.125), channel_id=1, source_target_pairs={{4,0},{8,4},{12,8},{16,12},{20,16},{24,20},{28,24},{32,28},{36,32}... | collective-permute-start | bytes 196616 | tf_op jit(solution)/shard_map/ppermute | solution.py:23
  442.8 6.5 %collective-permute-start.56 = (f32[4,1,32,128]{3,2,1,0:T(8,128)S(1)}, f32[4,1,32,128]{3,2,1,0:T(8,128)S(1)}, u32[]{:S(2)}, u32[]{:S(2)}) collective-permute-start(f32[4,1,32,128]{3,2,1,0:T(8,128)S(1)} %get-tuple-element.124), channel_id=1, source_target_pairs={{0,4},{4,8},{8,12},{12,16},{16,20},{20,24},{24,28},{28,32},{32,36}... | collective-permute-start | bytes 196616 | tf_op jit(solution)/shard_map/ppermute | solution.py:20
  449.3 8.0 %collective-permute-start.59 = (f32[4,6,1,128]{3,2,1,0:T(1,128)S(1)}, f32[4,6,1,128]{3,2,1,0:T(1,128)S(1)}, u32[]{:S(2)}, u32[]{:S(2)}) collective-permute-start(f32[4,6,1,128]{3,2,1,0:T(1,128)S(1)} %get-tuple-element.95), channel_id=1, source_target_pairs={{1,0},{2,1},{3,2},{5,4},{6,5},{7,6},{9,8},{10,9},{11,10},{13,12},{... | collective-permute-start | bytes 36872 | tf_op jit(solution)/shard_map/ppermute | solution.py:23
  451.2 7.4 %collective-permute-start.58 = (f32[4,6,1,128]{3,2,1,0:T(1,128)S(1)}, f32[4,6,1,128]{3,2,1,0:T(1,128)S(1)}, u32[]{:S(2)}, u32[]{:S(2)}) collective-permute-start(f32[4,6,1,128]{3,2,1,0:T(1,128)S(1)} %get-tuple-element.94), channel_id=1, source_target_pairs={{0,1},{1,2},{2,3},{4,5},{5,6},{6,7},{8,9},{9,10},{10,11},{12,13},{... | collective-permute-start | bytes 36872 | tf_op jit(solution)/shard_map/ppermute | solution.py:20
  459.1 7.1 %collective-permute-start.61 = (f32[8,1,32,128]{3,2,1,0:T(8,128)S(1)}, f32[8,1,32,128]{3,2,1,0:T(8,128)S(1)}, u32[]{:S(2)}, u32[]{:S(2)}) collective-permute-start(f32[8,1,32,128]{3,2,1,0:T(8,128)S(1)} %get-tuple-element.91), channel_id=1, source_target_pairs={{4,0},{8,4},{12,8},{16,12},{20,16},{24,20},{28,24},{32,28},{36,32}... | collective-permute-start | bytes 393224 | tf_op jit(solution)/shard_map/ppermute | solution.py:23
  460.4 6.7 %collective-permute-start.60 = (f32[8,1,32,128]{3,2,1,0:T(8,128)S(1)}, f32[8,1,32,128]{3,2,1,0:T(8,128)S(1)}, u32[]{:S(2)}, u32[]{:S(2)}) collective-permute-start(f32[8,1,32,128]{3,2,1,0:T(8,128)S(1)} %get-tuple-element.90), channel_id=1, source_target_pairs={{0,4},{4,8},{8,12},{12,16},{16,20},{20,24},{24,28},{28,32},{32,36}... | collective-permute-start | bytes 393224 | tf_op jit(solution)/shard_map/ppermute | solution.py:20
  467.2 8.8 %collective-permute-start.63 = (f32[8,6,1,128]{3,2,1,0:T(1,128)S(1)}, f32[8,6,1,128]{3,2,1,0:T(1,128)S(1)}, u32[]{:S(2)}, u32[]{:S(2)}) collective-permute-start(f32[8,6,1,128]{3,2,1,0:T(1,128)S(1)} %get-tuple-element.83), channel_id=1, source_target_pairs={{1,0},{2,1},{3,2},{5,4},{6,5},{7,6},{9,8},{10,9},{11,10},{13,12},{... | collective-permute-start | bytes 73736 | tf_op jit(solution)/shard_map/ppermute | solution.py:23
  469.2 7.5 %collective-permute-start.62 = (f32[8,6,1,128]{3,2,1,0:T(1,128)S(1)}, f32[8,6,1,128]{3,2,1,0:T(1,128)S(1)}, u32[]{:S(2)}, u32[]{:S(2)}) collective-permute-start(f32[8,6,1,128]{3,2,1,0:T(1,128)S(1)} %get-tuple-element.82), channel_id=1, source_target_pairs={{0,1},{1,2},{2,3},{4,5},{5,6},{6,7},{8,9},{9,10},{10,11},{12,13},{... | collective-permute-start | bytes 73736 | tf_op jit(solution)/shard_map/ppermute | solution.py:20
  (22 other events, 714.6 us)
Sparse Core Ops, SparseCore 0:
  477.9 105.9 all-reduce.20
where the time goes:
time: 595 us; the launch traced here: 592 us
  starting transfers between devices  224 us (38%)
  blocking collectives  174 us (29%)
  waiting for transfers between devices  153 us (26%)
  other arithmetic  15 us (3%)
  between operations  14.6 us (2%)
  local copies, waits for them, and re-layouts  12.1 us (2%)
    ppermute x32, starting transfers between devices, padded_2(): lax.ppermute(lax.slice_in_dim(block, block.shape[dim] - width, None, axis...  166 us
    psum x1, blocking collectives, body(): predicted = lax.psum(local_values, ('gx', 'gy'))  145 us
    psum x1, waiting for transfers between devices, reduce_groups(): summed = lax.psum(partial_value, 'src')  106 us
    ppermute x32, starting transfers between devices, padded_2(): lax.ppermute(lax.slice_in_dim(block, 0, width, axis=dim), axis, backward)  58.2 us
    all_gather x1, blocking collectives, body(): panel = lax.all_gather(conductivity, 'src', axis=2, tiled=True)  29 us
    ppermute x32, waiting for transfers between devices, padded_2(): lax.ppermute(lax.slice_in_dim(block, block.shape[dim] - width, None, axis...  24.7 us
    ppermute x32, waiting for transfers between devices, padded_2(): lax.ppermute(lax.slice_in_dim(block, 0, width, axis=dim), axis, backward)  22 us
  transfers between devices with their start and end apart: 65, of which 24 were waited for; matrix products, arithmetic and copies ran while one was open for 3% of the time, Pallas kernels for 0%

commit v1 on v0

--- a/solution.py
+++ b/solution.py
@@ -137,7 +137,7 @@
     local_values = jnp.dot(
         top, pickup.T, precision=lax.Precision.HIGHEST, preferred_element_type=jnp.float32
     )
-    predicted = lax.psum(local_values, ("gx", "gy"))
+    predicted = lax.psum(lax.psum(local_values, "gx"), "gy")
     misfit = predicted - rows_observed
     back = jnp.dot(
         misfit, pickup, precision=lax.Precision.HIGHEST, preferred_element_type=jnp.float32

time: 595 us -> 488 us (0.82)
  blocking collectives: 174 us -> 72.3 us
  waiting for transfers between devices: 153 us -> 147 us
    psum x1 -> x2, blocking collectives: 145 us -> 43.3 us  [body(): predicted = lax.psum(lax.psum(local_values, 'gx'), 'gy')]
where the time goes in v1:
time: 488 us; the launch traced here: 486 us
  starting transfers between devices  224 us (46%)
  waiting for transfers between devices  147 us (30%)
  blocking collectives  72.3 us (15%)
  other arithmetic  15 us (3%)
  between operations  14.6 us (3%)
  local copies, waits for them, and re-layouts  12.1 us (2%)
    ppermute x32, starting transfers between devices, padded_2(): lax.ppermute(lax.slice_in_dim(block, block.shape[dim] - width, None, axis...  167 us
    psum x1, waiting for transfers between devices, reduce_groups(): summed = lax.psum(partial_value, 'src')  101 us
    ppermute x32, starting transfers between devices, padded_2(): lax.ppermute(lax.slice_in_dim(block, 0, width, axis=dim), axis, backward)  57.9 us
    psum x2, blocking collectives, body(): predicted = lax.psum(lax.psum(local_values, 'gx'), 'gy')  43.3 us
    all_gather x1, blocking collectives, body(): panel = lax.all_gather(conductivity, 'src', axis=2, tiled=True)  29 us
    ppermute x32, waiting for transfers between devices, padded_2(): lax.ppermute(lax.slice_in_dim(block, block.shape[dim] - width, None, axis...  24.4 us
    ppermute x32, waiting for transfers between devices, padded_2(): lax.ppermute(lax.slice_in_dim(block, 0, width, axis=dim), axis, backward)  22 us
  transfers between devices with their start and end apart: 65, of which 24 were waited for; matrix products, arithmetic and copies ran while one was open for 3% of the time, Pallas kernels for 0%

profile of v1, /device:TPU:16, one launch (start us, length us, event | category | flops | bytes accessed | tf_op | source)
XLA Modules:
  0.0 486.2 jit_solution(16950973486809533254)
XLA Ops:
  7.3 29.0 %all_gather.3 = f32[4,32,128]{1,0,2:T(4,128)S(1)} all-gather(f32[4,32,16]{1,0,2:T(4,128)S(1)} %copy.69), channel_id=1, replica_groups=mesh['src'=8,'gx'=16,'gy'=4] {'src'}, dimensions={2}, use_global_device_ids=true | all-gather | bytes 73728 | tf_op jit(solution)/shard_map/all_gather | solution.py:104
  37.8 3.0 collective-permute-start
  40.9 3.9 collective-permute-start.4
  50.0 5.4 %collective-permute-start.3 = (f32[1,6,1,128]{2,1,3,0:T(8,128)S(1)}, f32[1,6,1,128]{2,1,3,0:T(8,128)S(1)}, u32[]{:S(2)}, u32[]{:S(2)}) collective-permute-start(f32[1,6,1,128]{2,1,3,0:T(8,128)S(1)} %get-tuple-element.93), channel_id=1, source_target_pairs={{1,0},{2,1},{3,2},{5,4},{6,5},{7,6},{9,8},{10,9},{11,10},{13,12},{... | collective-permute-start | bytes 9224 | tf_op jit(solution)/shard_map/ppermute | solution.py:23
  55.4 2.6 collective-permute-start.2
  58.0 21.9 %collective-permute-done.3 = f32[1,6,1,128]{2,1,3,0:T(8,128)S(1)} collective-permute-done((f32[1,6,1,128]{2,1,3,0:T(8,128)S(1)}, f32[1,6,1,128]{2,1,3,0:T(8,128)S(1)}, u32[]{:S(2)}, u32[]{:S(2)}) %collective-permute-start.3) | collective-permute-done | bytes 3104 | tf_op jit(solution)/shard_map/ppermute | solution.py:23
  80.5 1.8 fusion.293
  82.3 2.3 collective-permute-start.7
  84.7 5.6 %collective-permute-start.6 = (f32[4,6,1,128]{3,2,1,0:T(1,128)S(1)}, f32[4,6,1,128]{3,2,1,0:T(1,128)S(1)}, u32[]{:S(2)}, u32[]{:S(2)}) collective-permute-start(f32[4,6,1,128]{3,2,1,0:T(1,128)S(1)} %get-tuple-element.120), channel_id=1, source_target_pairs={{0,1},{1,2},{2,3},{4,5},{5,6},{6,7},{8,9},{9,10},{10,11},{12,13},{... | collective-permute-start | bytes 36872 | tf_op jit(solution)/shard_map/ppermute | solution.py:20
  90.3 2.0 add_divide_fusion
  96.5 3.0 collective-permute-start.8
  100.5 1.9 collective-permute-start.11
  102.4 6.0 %collective-permute-start.10 = (f32[4,6,1,128]{3,2,1,0:T(1,128)S(1)}, f32[4,6,1,128]{3,2,1,0:T(1,128)S(1)}, u32[]{:S(2)}, u32[]{:S(2)}) collective-permute-start(f32[4,6,1,128]{3,2,1,0:T(1,128)S(1)} %get-tuple-element.118), channel_id=1, source_target_pairs={{0,1},{1,2},{2,3},{4,5},{5,6},{6,7},{8,9},{9,10},{10,11},{12,13},{... | collective-permute-start | bytes 36872 | tf_op jit(solution)/shard_map/ppermute | solution.py:20
  108.5 1.4 collective-permute-done.10
  111.4 5.8 %collective-permute-start.12 = (f32[4,1,32,128]{3,2,1,0:T(8,128)S(1)}, f32[4,1,32,128]{3,2,1,0:T(8,128)S(1)}, u32[]{:S(2)}, u32[]{:S(2)}) collective-permute-start(f32[4,1,32,128]{3,2,1,0:T(8,128)S(1)} %get-tuple-element.146), channel_id=1, source_target_pairs={{0,4},{4,8},{8,12},{12,16},{16,20},{20,24},{24,28},{28,32},{32,36}... | collective-permute-start | bytes 196616 | tf_op jit(solution)/shard_map/ppermute | solution.py:20
  118.2 1.9 collective-permute-start.15
  120.1 6.0 %collective-permute-start.14 = (f32[4,6,1,128]{3,2,1,0:T(1,128)S(1)}, f32[4,6,1,128]{3,2,1,0:T(1,128)S(1)}, u32[]{:S(2)}, u32[]{:S(2)}) collective-permute-start(f32[4,6,1,128]{3,2,1,0:T(1,128)S(1)} %get-tuple-element.116), channel_id=1, source_target_pairs={{0,1},{1,2},{2,3},{4,5},{5,6},{6,7},{8,9},{9,10},{10,11},{12,13},{... | collective-permute-start | bytes 36872 | tf_op jit(solution)/shard_map/ppermute | solution.py:20
  126.2 1.4 collective-permute-done.14
  127.8 1.4 collective-permute-start.17
  129.3 5.9 %collective-permute-start.16 = (f32[4,1,32,128]{3,2,1,0:T(8,128)S(1)}, f32[4,1,32,128]{3,2,1,0:T(8,128)S(1)}, u32[]{:S(2)}, u32[]{:S(2)}) collective-permute-start(f32[4,1,32,128]{3,2,1,0:T(8,128)S(1)} %get-tuple-element.144), channel_id=1, source_target_pairs={{0,4},{4,8},{8,12},{12,16},{16,20},{20,24},{24,28},{28,32},{32,36}... | collective-permute-start | bytes 196616 | tf_op jit(solution)/shard_map/ppermute | solution.py:20
  136.1 1.9 collective-permute-start.19
  138.0 6.0 %collective-permute-start.18 = (f32[4,6,1,128]{3,2,1,0:T(1,128)S(1)}, f32[4,6,1,128]{3,2,1,0:T(1,128)S(1)}, u32[]{:S(2)}, u32[]{:S(2)}) collective-permute-start(f32[4,6,1,128]{3,2,1,0:T(1,128)S(1)} %get-tuple-element.114), channel_id=1, source_target_pairs={{0,1},{1,2},{2,3},{4,5},{5,6},{6,7},{8,9},{9,10},{10,11},{12,13},{... | collective-permute-start | bytes 36872 | tf_op jit(solution)/shard_map/ppermute | solution.py:20
  144.7 5.5 %collective-permute-start.32 = (f32[4,1,32,128]{3,2,1,0:T(8,128)}, f32[4,1,32,128]{3,2,1,0:T(8,128)S(1)}, u32[]{:S(2)}, u32[]{:S(2)}) collective-permute-start(f32[4,1,32,128]{3,2,1,0:T(8,128)} %get-tuple-element.137), channel_id=1, source_target_pairs={{0,4},{4,8},{8,12},{12,16},{16,20},{20,24},{24,28},{28,32},{32,36}... | collective-permute-start | bytes 196616 | tf_op jit(solution)/shard_map/ppermute | solution.py:20
  153.2 5.8 %collective-permute-start.20 = (f32[4,1,32,128]{3,2,1,0:T(8,128)S(1)}, f32[4,1,32,128]{3,2,1,0:T(8,128)S(1)}, u32[]{:S(2)}, u32[]{:S(2)}) collective-permute-start(f32[4,1,32,128]{3,2,1,0:T(8,128)S(1)} %get-tuple-element.142), channel_id=1, source_target_pairs={{0,4},{4,8},{8,12},{12,16},{16,20},{20,24},{24,28},{28,32},{32,36}... | collective-permute-start | bytes 196616 | tf_op jit(solution)/shard_map/ppermute | solution.py:20
  160.5 1.9 collective-permute-start.23
  162.4 6.0 %collective-permute-start.22 = (f32[4,6,1,128]{3,2,1,0:T(1,128)}, f32[4,6,1,128]{3,2,1,0:T(1,128)}, u32[]{:S(2)}, u32[]{:S(2)}) collective-permute-start(f32[4,6,1,128]{3,2,1,0:T(1,128)} %get-tuple-element.112), channel_id=1, source_target_pairs={{0,1},{1,2},{2,3},{4,5},{5,6},{6,7},{8,9},{9,10},{10,11},{12,13},{... | collective-permute-start | bytes 36872 | tf_op jit(solution)/shard_map/ppermute | solution.py:20
  172.6 4.1 collective-permute-start.24
  177.7 1.9 collective-permute-start.27
  179.6 6.0 %collective-permute-start.26 = (f32[4,6,1,128]{3,2,1,0:T(1,128)S(1)}, f32[4,6,1,128]{3,2,1,0:T(1,128)S(1)}, u32[]{:S(2)}, u32[]{:S(2)}) collective-permute-start(f32[4,6,1,128]{3,2,1,0:T(1,128)S(1)} %get-tuple-element.110), channel_id=1, source_target_pairs={{0,1},{1,2},{2,3},{4,5},{5,6},{6,7},{8,9},{9,10},{10,11},{12,13},{... | collective-permute-start | bytes 36872 | tf_op jit(solution)/shard_map/ppermute | solution.py:20
  188.6 5.2 %collective-permute-start.28 = (f32[4,1,32,128]{3,2,1,0:T(8,128)S(1)}, f32[4,1,32,128]{3,2,1,0:T(8,128)S(1)}, u32[]{:S(2)}, u32[]{:S(2)}) collective-permute-start(f32[4,1,32,128]{3,2,1,0:T(8,128)S(1)} %get-tuple-element.138), channel_id=1, source_target_pairs={{0,4},{4,8},{8,12},{12,16},{16,20},{20,24},{24,28},{28,32},{32,36}... | collective-permute-start | bytes 196616 | tf_op jit(solution)/shard_map/ppermute | solution.py:20
  194.7 1.9 collective-permute-start.31
  196.6 6.0 %collective-permute-start.30 = (f32[4,6,1,128]{3,2,1,0:T(1,128)S(1)}, f32[4,6,1,128]{3,2,1,0:T(1,128)S(1)}, u32[]{:S(2)}, u32[]{:S(2)}) collective-permute-start(f32[4,6,1,128]{3,2,1,0:T(1,128)S(1)} %get-tuple-element.108), channel_id=1, source_target_pairs={{0,1},{1,2},{2,3},{4,5},{5,6},{6,7},{8,9},{9,10},{10,11},{12,13},{... | collective-permute-start | bytes 36872 | tf_op jit(solution)/shard_map/ppermute | solution.py:20
  202.7 1.9 collective-permute-start.35
  204.6 6.0 %collective-permute-start.34 = (f32[4,6,1,128]{3,2,1,0:T(1,128)S(1)}, f32[4,6,1,128]{3,2,1,0:T(1,128)S(1)}, u32[]{:S(2)}, u32[]{:S(2)}) collective-permute-start(f32[4,6,1,128]{3,2,1,0:T(1,128)S(1)} %get-tuple-element.106), channel_id=1, source_target_pairs={{0,1},{1,2},{2,3},{4,5},{5,6},{6,7},{8,9},{9,10},{10,11},{12,13},{... | collective-permute-start | bytes 36872 | tf_op jit(solution)/shard_map/ppermute | solution.py:20
  212.4 34.2 %psum.21 = f32[4,128]{1,0:T(4,128)S(1)} all-reduce(f32[4,128]{1,0:T(4,128)S(1)} %fusion.300), channel_id=1, replica_groups=mesh['src'=8,'gx'=16,'gy'=4] {'gx'}, use_global_device_ids=true, to_apply=%region_0.1 | all-reduce | flops 512 | bytes 4096 | tf_op jit(solution)/shard_map/psum | solution.py:140
  246.5 9.1 %psum.22 = f32[4,128]{1,0:T(4,128)S(1)} all-reduce(f32[4,128]{1,0:T(4,128)S(1)} %psum.21), channel_id=1, replica_groups=mesh['src'=8,'gx'=16,'gy'=4] {'gy'}, use_global_device_ids=true, to_apply=%region_1.2 | all-reduce | flops 512 | bytes 4096 | tf_op jit(solution)/shard_map/psum | solution.py:140
  258.6 3.0 collective-permute-start.36
  262.6 4.3 collective-permute-start.39
  266.9 3.6 collective-permute-start.38
  270.5 2.9 collective-permute-done.38
  275.0 3.0 collective-permute-start.40
  279.0 1.9 collective-permute-start.43
  280.9 6.0 %collective-permute-start.42 = (f32[4,6,1,128]{3,2,1,0:T(1,128)S(1)}, f32[4,6,1,128]{3,2,1,0:T(1,128)S(1)}, u32[]{:S(2)}, u32[]{:S(2)}) collective-permute-start(f32[4,6,1,128]{3,2,1,0:T(1,128)S(1)} %get-tuple-element.102), channel_id=1, source_target_pairs={{0,1},{1,2},{2,3},{4,5},{5,6},{6,7},{8,9},{9,10},{10,11},{12,13},{... | collective-permute-start | bytes 36872 | tf_op jit(solution)/shard_map/ppermute | solution.py:20
  286.9 1.4 collective-permute-done.42
  289.9 5.0 %collective-permute-start.44 = (f32[4,1,32,128]{3,2,1,0:T(8,128)S(1)}, f32[4,1,32,128]{3,2,1,0:T(8,128)S(1)}, u32[]{:S(2)}, u32[]{:S(2)}) collective-permute-start(f32[4,1,32,128]{3,2,1,0:T(8,128)S(1)} %get-tuple-element.130), channel_id=1, source_target_pairs={{0,4},{4,8},{8,12},{12,16},{16,20},{20,24},{24,28},{28,32},{32,36}... | collective-permute-start | bytes 196616 | tf_op jit(solution)/shard_map/ppermute | solution.py:20
  295.7 1.9 collective-permute-start.47
  297.6 6.0 %collective-permute-start.46 = (f32[4,6,1,128]{3,2,1,0:T(1,128)S(1)}, f32[4,6,1,128]{3,2,1,0:T(1,128)S(1)}, u32[]{:S(2)}, u32[]{:S(2)}) collective-permute-start(f32[4,6,1,128]{3,2,1,0:T(1,128)S(1)} %get-tuple-element.100), channel_id=1, source_target_pairs={{0,1},{1,2},{2,3},{4,5},{5,6},{6,7},{8,9},{9,10},{10,11},{12,13},{... | collective-permute-start | bytes 36872 | tf_op jit(solution)/shard_map/ppermute | solution.py:20
  303.6 1.4 collective-permute-done.46
  306.6 6.0 %collective-permute-start.48 = (f32[4,1,32,128]{3,2,1,0:T(8,128)S(1)}, f32[4,1,32,128]{3,2,1,0:T(8,128)S(1)}, u32[]{:S(2)}, u32[]{:S(2)}) collective-permute-start(f32[4,1,32,128]{3,2,1,0:T(8,128)S(1)} %get-tuple-element.128), channel_id=1, source_target_pairs={{0,4},{4,8},{8,12},{12,16},{16,20},{20,24},{24,28},{28,32},{32,36}... | collective-permute-start | bytes 196616 | tf_op jit(solution)/shard_map/ppermute | solution.py:20
  313.5 1.9 collective-permute-start.51
  315.5 6.0 %collective-permute-start.50 = (f32[4,6,1,128]{3,2,1,0:T(1,128)S(1)}, f32[4,6,1,128]{3,2,1,0:T(1,128)S(1)}, u32[]{:S(2)}, u32[]{:S(2)}) collective-permute-start(f32[4,6,1,128]{3,2,1,0:T(1,128)S(1)} %get-tuple-element.98), channel_id=1, source_target_pairs={{0,1},{1,2},{2,3},{4,5},{5,6},{6,7},{8,9},{9,10},{10,11},{12,13},{... | collective-permute-start | bytes 36872 | tf_op jit(solution)/shard_map/ppermute | solution.py:20
  321.5 1.4 collective-permute-done.50
  324.5 5.6 %collective-permute-start.52 = (f32[4,1,32,128]{3,2,1,0:T(8,128)S(1)}, f32[4,1,32,128]{3,2,1,0:T(8,128)S(1)}, u32[]{:S(2)}, u32[]{:S(2)}) collective-permute-start(f32[4,1,32,128]{3,2,1,0:T(8,128)S(1)} %get-tuple-element.126), channel_id=1, source_target_pairs={{0,4},{4,8},{8,12},{12,16},{16,20},{20,24},{24,28},{28,32},{32,36}... | collective-permute-start | bytes 196616 | tf_op jit(solution)/shard_map/ppermute | solution.py:20
  331.0 1.9 collective-permute-start.55
  332.9 6.0 %collective-permute-start.54 = (f32[4,6,1,128]{3,2,1,0:T(1,128)S(1)}, f32[4,6,1,128]{3,2,1,0:T(1,128)S(1)}, u32[]{:S(2)}, u32[]{:S(2)}) collective-permute-start(f32[4,6,1,128]{3,2,1,0:T(1,128)S(1)} %get-tuple-element.96), channel_id=1, source_target_pairs={{0,1},{1,2},{2,3},{4,5},{5,6},{6,7},{8,9},{9,10},{10,11},{12,13},{... | collective-permute-start | bytes 36872 | tf_op jit(solution)/shard_map/ppermute | solution.py:20
  339.0 1.4 collective-permute-done.54
  342.0 5.6 %collective-permute-start.56 = (f32[4,1,32,128]{3,2,1,0:T(8,128)S(1)}, f32[4,1,32,128]{3,2,1,0:T(8,128)S(1)}, u32[]{:S(2)}, u32[]{:S(2)}) collective-permute-start(f32[4,1,32,128]{3,2,1,0:T(8,128)S(1)} %get-tuple-element.124), channel_id=1, source_target_pairs={{0,4},{4,8},{8,12},{12,16},{16,20},{20,24},{24,28},{28,32},{32,36}... | collective-permute-start | bytes 196616 | tf_op jit(solution)/shard_map/ppermute | solution.py:20
  348.5 1.9 collective-permute-start.59
  350.4 6.0 %collective-permute-start.58 = (f32[4,6,1,128]{3,2,1,0:T(1,128)S(1)}, f32[4,6,1,128]{3,2,1,0:T(1,128)S(1)}, u32[]{:S(2)}, u32[]{:S(2)}) collective-permute-start(f32[4,6,1,128]{3,2,1,0:T(1,128)S(1)} %get-tuple-element.94), channel_id=1, source_target_pairs={{0,1},{1,2},{2,3},{4,5},{5,6},{6,7},{8,9},{9,10},{10,11},{12,13},{... | collective-permute-start | bytes 36872 | tf_op jit(solution)/shard_map/ppermute | solution.py:20
  356.5 1.4 collective-permute-done.58
  359.6 5.7 %collective-permute-start.60 = (f32[8,1,32,128]{3,2,1,0:T(8,128)S(1)}, f32[8,1,32,128]{3,2,1,0:T(8,128)S(1)}, u32[]{:S(2)}, u32[]{:S(2)}) collective-permute-start(f32[8,1,32,128]{3,2,1,0:T(8,128)S(1)} %get-tuple-element.90), channel_id=1, source_target_pairs={{0,4},{4,8},{8,12},{12,16},{16,20},{20,24},{24,28},{28,32},{32,36}... | collective-permute-start | bytes 393224 | tf_op jit(solution)/shard_map/ppermute | solution.py:20
  366.4 2.1 collective-permute-start.63
  368.4 6.0 %collective-permute-start.62 = (f32[8,6,1,128]{3,2,1,0:T(1,128)S(1)}, f32[8,6,1,128]{3,2,1,0:T(1,128)S(1)}, u32[]{:S(2)}, u32[]{:S(2)}) collective-permute-start(f32[8,6,1,128]{3,2,1,0:T(1,128)S(1)} %get-tuple-element.82), channel_id=1, source_target_pairs={{0,1},{1,2},{2,3},{4,5},{5,6},{6,7},{8,9},{9,10},{10,11},{12,13},{... | collective-permute-start | bytes 73736 | tf_op jit(solution)/shard_map/ppermute | solution.py:20
  377.0 100.7 %all-reduce.21.cloned.1.call-done = f32[4,32,128]{2,1,0:T(8,128)} async-done(((f32[4,32,128]{2,1,0:T(8,128)}), f32[4,32,128]{2,1,0:T(8,128)}) %all-reduce.21.cloned.1.call-update) | async-done | bytes 65552 | tf_op jit(solution)/shard_map/psum | solution.py:99
  (204 shorter events, 55.3 us)
Async XLA Ops:
  6.5 471.2 %all-reduce.21.cloned.1.call-start = ((), (), s32[]{:S(2)}) async-start(), calls=%async_computation | async-start | bytes 131072 | tf_op jit(solution)/shard_map/psum | solution.py:99
  36.5 13.1 %collective-permute-start.1 = (f32[1,1,32,128]{2,1,3,0:T(1,128)S(1)}, f32[1,1,32,128]{2,1,3,0:T(1,128)S(1)}, u32[]{:S(2)}, u32[]{:S(2)}) collective-permute-start(f32[1,1,32,128]{2,1,3,0:T(1,128)S(1)} %get-tuple-element.153), channel_id=1, source_target_pairs={{4,0},{8,4},{12,8},{16,12},{20,16},{24,20},{28,24},{32,28},{36,32}... | collective-permute-start | bytes 49160 | tf_op jit(solution)/shard_map/ppermute | solution.py:23
  37.8 11.8 %collective-permute-start = (f32[1,1,32,128]{2,1,3,0:T(1,128)S(1)}, f32[1,1,32,128]{2,1,3,0:T(1,128)S(1)}, u32[]{:S(2)}, u32[]{:S(2)}) collective-permute-start(f32[1,1,32,128]{2,1,3,0:T(1,128)S(1)} %get-tuple-element.152), channel_id=1, source_target_pairs={{0,4},{4,8},{8,12},{12,16},{16,20},{20,24},{24,28},{28,32},{32,36}... | collective-permute-start | bytes 49160 | tf_op jit(solution)/shard_map/ppermute | solution.py:20
  40.9 41.4 %collective-permute-start.4 = (f32[4,1,32,128]{3,2,1,0:T(8,128)S(1)}, f32[4,1,32,128]{3,2,1,0:T(8,128)S(1)}, u32[]{:S(2)}, u32[]{:S(2)}) collective-permute-start(f32[4,1,32,128]{3,2,1,0:T(8,128)S(1)} %get-tuple-element.151), channel_id=1, source_target_pairs={{0,4},{4,8},{8,12},{12,16},{16,20},{20,24},{24,28},{28,32},{32,36}... | collective-permute-start | bytes 196616 | tf_op jit(solution)/shard_map/ppermute | solution.py:20
  44.8 37.5 %collective-permute-start.5 = (f32[4,1,32,128]{3,2,1,0:T(8,128)S(1)}, f32[4,1,32,128]{3,2,1,0:T(8,128)S(1)}, u32[]{:S(2)}, u32[]{:S(2)}) collective-permute-start(f32[4,1,32,128]{3,2,1,0:T(8,128)S(1)} %get-tuple-element.150), channel_id=1, source_target_pairs={{4,0},{8,4},{12,8},{16,12},{20,16},{24,20},{28,24},{32,28},{36,32}... | collective-permute-start | bytes 196616 | tf_op jit(solution)/shard_map/ppermute | solution.py:23
  50.0 29.9 %collective-permute-start.3 = (f32[1,6,1,128]{2,1,3,0:T(8,128)S(1)}, f32[1,6,1,128]{2,1,3,0:T(8,128)S(1)}, u32[]{:S(2)}, u32[]{:S(2)}) collective-permute-start(f32[1,6,1,128]{2,1,3,0:T(8,128)S(1)} %get-tuple-element.93), channel_id=1, source_target_pairs={{1,0},{2,1},{3,2},{5,4},{6,5},{7,6},{9,8},{10,9},{11,10},{13,12},{... | collective-permute-start | bytes 9224 | tf_op jit(solution)/shard_map/ppermute | solution.py:23
  55.4 24.5 %collective-permute-start.2 = (f32[1,6,1,128]{2,1,3,0:T(8,128)S(1)}, f32[1,6,1,128]{2,1,3,0:T(8,128)S(1)}, u32[]{:S(2)}, u32[]{:S(2)}) collective-permute-start(f32[1,6,1,128]{2,1,3,0:T(8,128)S(1)} %get-tuple-element.92), channel_id=1, source_target_pairs={{0,1},{1,2},{2,3},{4,5},{5,6},{6,7},{8,9},{9,10},{10,11},{12,13},{... | collective-permute-start | bytes 9224 | tf_op jit(solution)/shard_map/ppermute | solution.py:20
  82.3 11.8 %collective-permute-start.7 = (f32[4,6,1,128]{3,2,1,0:T(1,128)S(1)}, f32[4,6,1,128]{3,2,1,0:T(1,128)S(1)}, u32[]{:S(2)}, u32[]{:S(2)}) collective-permute-start(f32[4,6,1,128]{3,2,1,0:T(1,128)S(1)} %get-tuple-element.121), channel_id=1, source_target_pairs={{1,0},{2,1},{3,2},{5,4},{6,5},{7,6},{9,8},{10,9},{11,10},{13,12},{... | collective-permute-start | bytes 36872 | tf_op jit(solution)/shard_map/ppermute | solution.py:23
  84.7 9.4 %collective-permute-start.6 = (f32[4,6,1,128]{3,2,1,0:T(1,128)S(1)}, f32[4,6,1,128]{3,2,1,0:T(1,128)S(1)}, u32[]{:S(2)}, u32[]{:S(2)}) collective-permute-start(f32[4,6,1,128]{3,2,1,0:T(1,128)S(1)} %get-tuple-element.120), channel_id=1, source_target_pairs={{0,1},{1,2},{2,3},{4,5},{5,6},{6,7},{8,9},{9,10},{10,11},{12,13},{... | collective-permute-start | bytes 36872 | tf_op jit(solution)/shard_map/ppermute | solution.py:20
  95.2 4.3 collective-permute-start.9
  96.5 3.9 collective-permute-start.8
  100.5 8.0 %collective-permute-start.11 = (f32[4,6,1,128]{3,2,1,0:T(1,128)S(1)}, f32[4,6,1,128]{3,2,1,0:T(1,128)S(1)}, u32[]{:S(2)}, u32[]{:S(2)}) collective-permute-start(f32[4,6,1,128]{3,2,1,0:T(1,128)S(1)} %get-tuple-element.119), channel_id=1, source_target_pairs={{1,0},{2,1},{3,2},{5,4},{6,5},{7,6},{9,8},{10,9},{11,10},{13,12},{... | collective-permute-start | bytes 36872 | tf_op jit(solution)/shard_map/ppermute | solution.py:23
  102.4 7.4 %collective-permute-start.10 = (f32[4,6,1,128]{3,2,1,0:T(1,128)S(1)}, f32[4,6,1,128]{3,2,1,0:T(1,128)S(1)}, u32[]{:S(2)}, u32[]{:S(2)}) collective-permute-start(f32[4,6,1,128]{3,2,1,0:T(1,128)S(1)} %get-tuple-element.118), channel_id=1, source_target_pairs={{0,1},{1,2},{2,3},{4,5},{5,6},{6,7},{8,9},{9,10},{10,11},{12,13},{... | collective-permute-start | bytes 36872 | tf_op jit(solution)/shard_map/ppermute | solution.py:20
  110.1 7.1 %collective-permute-start.13 = (f32[4,1,32,128]{3,2,1,0:T(8,128)S(1)}, f32[4,1,32,128]{3,2,1,0:T(8,128)S(1)}, u32[]{:S(2)}, u32[]{:S(2)}) collective-permute-start(f32[4,1,32,128]{3,2,1,0:T(8,128)S(1)} %get-tuple-element.147), channel_id=1, source_target_pairs={{4,0},{8,4},{12,8},{16,12},{20,16},{24,20},{28,24},{32,28},{36,32}... | collective-permute-start | bytes 196616 | tf_op jit(solution)/shard_map/ppermute | solution.py:23
  111.4 6.7 %collective-permute-start.12 = (f32[4,1,32,128]{3,2,1,0:T(8,128)S(1)}, f32[4,1,32,128]{3,2,1,0:T(8,128)S(1)}, u32[]{:S(2)}, u32[]{:S(2)}) collective-permute-start(f32[4,1,32,128]{3,2,1,0:T(8,128)S(1)} %get-tuple-element.146), channel_id=1, source_target_pairs={{0,4},{4,8},{8,12},{12,16},{16,20},{20,24},{24,28},{28,32},{32,36}... | collective-permute-start | bytes 196616 | tf_op jit(solution)/shard_map/ppermute | solution.py:20
  118.2 8.0 %collective-permute-start.15 = (f32[4,6,1,128]{3,2,1,0:T(1,128)S(1)}, f32[4,6,1,128]{3,2,1,0:T(1,128)S(1)}, u32[]{:S(2)}, u32[]{:S(2)}) collective-permute-start(f32[4,6,1,128]{3,2,1,0:T(1,128)S(1)} %get-tuple-element.117), channel_id=1, source_target_pairs={{1,0},{2,1},{3,2},{5,4},{6,5},{7,6},{9,8},{10,9},{11,10},{13,12},{... | collective-permute-start | bytes 36872 | tf_op jit(solution)/shard_map/ppermute | solution.py:23
  120.1 7.4 %collective-permute-start.14 = (f32[4,6,1,128]{3,2,1,0:T(1,128)S(1)}, f32[4,6,1,128]{3,2,1,0:T(1,128)S(1)}, u32[]{:S(2)}, u32[]{:S(2)}) collective-permute-start(f32[4,6,1,128]{3,2,1,0:T(1,128)S(1)} %get-tuple-element.116), channel_id=1, source_target_pairs={{0,1},{1,2},{2,3},{4,5},{5,6},{6,7},{8,9},{9,10},{10,11},{12,13},{... | collective-permute-start | bytes 36872 | tf_op jit(solution)/shard_map/ppermute | solution.py:20
  127.8 7.3 %collective-permute-start.17 = (f32[4,1,32,128]{3,2,1,0:T(8,128)S(1)}, f32[4,1,32,128]{3,2,1,0:T(8,128)S(1)}, u32[]{:S(2)}, u32[]{:S(2)}) collective-permute-start(f32[4,1,32,128]{3,2,1,0:T(8,128)S(1)} %get-tuple-element.145), channel_id=1, source_target_pairs={{4,0},{8,4},{12,8},{16,12},{20,16},{24,20},{28,24},{32,28},{36,32}... | collective-permute-start | bytes 196616 | tf_op jit(solution)/shard_map/ppermute | solution.py:23
  129.3 6.8 %collective-permute-start.16 = (f32[4,1,32,128]{3,2,1,0:T(8,128)S(1)}, f32[4,1,32,128]{3,2,1,0:T(8,128)S(1)}, u32[]{:S(2)}, u32[]{:S(2)}) collective-permute-start(f32[4,1,32,128]{3,2,1,0:T(8,128)S(1)} %get-tuple-element.144), channel_id=1, source_target_pairs={{0,4},{4,8},{8,12},{12,16},{16,20},{20,24},{24,28},{28,32},{32,36}... | collective-permute-start | bytes 196616 | tf_op jit(solution)/shard_map/ppermute | solution.py:20
  136.1 15.5 %collective-permute-start.19 = (f32[4,6,1,128]{3,2,1,0:T(1,128)S(1)}, f32[4,6,1,128]{3,2,1,0:T(1,128)S(1)}, u32[]{:S(2)}, u32[]{:S(2)}) collective-permute-start(f32[4,6,1,128]{3,2,1,0:T(1,128)S(1)} %get-tuple-element.115), channel_id=1, source_target_pairs={{1,0},{2,1},{3,2},{5,4},{6,5},{7,6},{9,8},{10,9},{11,10},{13,12},{... | collective-permute-start | bytes 36872 | tf_op jit(solution)/shard_map/ppermute | solution.py:23
  138.0 13.6 %collective-permute-start.18 = (f32[4,6,1,128]{3,2,1,0:T(1,128)S(1)}, f32[4,6,1,128]{3,2,1,0:T(1,128)S(1)}, u32[]{:S(2)}, u32[]{:S(2)}) collective-permute-start(f32[4,6,1,128]{3,2,1,0:T(1,128)S(1)} %get-tuple-element.114), channel_id=1, source_target_pairs={{0,1},{1,2},{2,3},{4,5},{5,6},{6,7},{8,9},{9,10},{10,11},{12,13},{... | collective-permute-start | bytes 36872 | tf_op jit(solution)/shard_map/ppermute | solution.py:20
  144.7 32.1 %collective-permute-start.32 = (f32[4,1,32,128]{3,2,1,0:T(8,128)}, f32[4,1,32,128]{3,2,1,0:T(8,128)S(1)}, u32[]{:S(2)}, u32[]{:S(2)}) collective-permute-start(f32[4,1,32,128]{3,2,1,0:T(8,128)} %get-tuple-element.137), channel_id=1, source_target_pairs={{0,4},{4,8},{8,12},{12,16},{16,20},{20,24},{24,28},{28,32},{32,36}... | collective-permute-start | bytes 196616 | tf_op jit(solution)/shard_map/ppermute | solution.py:20
  150.2 43.6 %collective-permute-start.33 = (f32[4,1,32,128]{3,2,1,0:T(8,128)}, f32[4,1,32,128]{3,2,1,0:T(8,128)}, u32[]{:S(2)}, u32[]{:S(2)}) collective-permute-start(f32[4,1,32,128]{3,2,1,0:T(8,128)} %get-tuple-element.136), channel_id=1, source_target_pairs={{4,0},{8,4},{12,8},{16,12},{20,16},{24,20},{28,24},{32,28},{36,32}... | collective-permute-start | bytes 196616 | tf_op jit(solution)/shard_map/ppermute | solution.py:23
  151.9 7.7 %collective-permute-start.21 = (f32[4,1,32,128]{3,2,1,0:T(8,128)S(1)}, f32[4,1,32,128]{3,2,1,0:T(8,128)S(1)}, u32[]{:S(2)}, u32[]{:S(2)}) collective-permute-start(f32[4,1,32,128]{3,2,1,0:T(8,128)S(1)} %get-tuple-element.143), channel_id=1, source_target_pairs={{4,0},{8,4},{12,8},{16,12},{20,16},{24,20},{28,24},{32,28},{36,32}... | collective-permute-start | bytes 196616 | tf_op jit(solution)/shard_map/ppermute | solution.py:23
  153.2 6.7 %collective-permute-start.20 = (f32[4,1,32,128]{3,2,1,0:T(8,128)S(1)}, f32[4,1,32,128]{3,2,1,0:T(8,128)S(1)}, u32[]{:S(2)}, u32[]{:S(2)}) collective-permute-start(f32[4,1,32,128]{3,2,1,0:T(8,128)S(1)} %get-tuple-element.142), channel_id=1, source_target_pairs={{0,4},{4,8},{8,12},{12,16},{16,20},{20,24},{24,28},{28,32},{32,36}... | collective-permute-start | bytes 196616 | tf_op jit(solution)/shard_map/ppermute | solution.py:20
  160.5 9.8 %collective-permute-start.23 = (f32[4,6,1,128]{3,2,1,0:T(1,128)}, f32[4,6,1,128]{3,2,1,0:T(1,128)}, u32[]{:S(2)}, u32[]{:S(2)}) collective-permute-start(f32[4,6,1,128]{3,2,1,0:T(1,128)} %get-tuple-element.113), channel_id=1, source_target_pairs={{1,0},{2,1},{3,2},{5,4},{6,5},{7,6},{9,8},{10,9},{11,10},{13,12},{... | collective-permute-start | bytes 36872 | tf_op jit(solution)/shard_map/ppermute | solution.py:23
  162.4 7.9 %collective-permute-start.22 = (f32[4,6,1,128]{3,2,1,0:T(1,128)}, f32[4,6,1,128]{3,2,1,0:T(1,128)}, u32[]{:S(2)}, u32[]{:S(2)}) collective-permute-start(f32[4,6,1,128]{3,2,1,0:T(1,128)} %get-tuple-element.112), channel_id=1, source_target_pairs={{0,1},{1,2},{2,3},{4,5},{5,6},{6,7},{8,9},{9,10},{10,11},{12,13},{... | collective-permute-start | bytes 36872 | tf_op jit(solution)/shard_map/ppermute | solution.py:20
  171.3 5.5 %collective-permute-start.25 = (f32[4,1,32,128]{3,2,1,0:T(8,128)S(1)}, f32[4,1,32,128]{3,2,1,0:T(8,128)S(1)}, u32[]{:S(2)}, u32[]{:S(2)}) collective-permute-start(f32[4,1,32,128]{3,2,1,0:T(8,128)S(1)} %get-tuple-element.141), channel_id=1, source_target_pairs={{4,0},{8,4},{12,8},{16,12},{20,16},{24,20},{28,24},{32,28},{36,32}... | collective-permute-start | bytes 196616 | tf_op jit(solution)/shard_map/ppermute | solution.py:23
  172.6 5.0 %collective-permute-start.24 = (f32[4,1,32,128]{3,2,1,0:T(8,128)S(1)}, f32[4,1,32,128]{3,2,1,0:T(8,128)S(1)}, u32[]{:S(2)}, u32[]{:S(2)}) collective-permute-start(f32[4,1,32,128]{3,2,1,0:T(8,128)S(1)} %get-tuple-element.140), channel_id=1, source_target_pairs={{0,4},{4,8},{8,12},{12,16},{16,20},{20,24},{24,28},{28,32},{32,36}... | collective-permute-start | bytes 196616 | tf_op jit(solution)/shard_map/ppermute | solution.py:20
  177.7 8.0 %collective-permute-start.27 = (f32[4,6,1,128]{3,2,1,0:T(1,128)S(1)}, f32[4,6,1,128]{3,2,1,0:T(1,128)S(1)}, u32[]{:S(2)}, u32[]{:S(2)}) collective-permute-start(f32[4,6,1,128]{3,2,1,0:T(1,128)S(1)} %get-tuple-element.111), channel_id=1, source_target_pairs={{1,0},{2,1},{3,2},{5,4},{6,5},{7,6},{9,8},{10,9},{11,10},{13,12},{... | collective-permute-start | bytes 36872 | tf_op jit(solution)/shard_map/ppermute | solution.py:23
  179.6 7.4 %collective-permute-start.26 = (f32[4,6,1,128]{3,2,1,0:T(1,128)S(1)}, f32[4,6,1,128]{3,2,1,0:T(1,128)S(1)}, u32[]{:S(2)}, u32[]{:S(2)}) collective-permute-start(f32[4,6,1,128]{3,2,1,0:T(1,128)S(1)} %get-tuple-element.110), channel_id=1, source_target_pairs={{0,1},{1,2},{2,3},{4,5},{5,6},{6,7},{8,9},{9,10},{10,11},{12,13},{... | collective-permute-start | bytes 36872 | tf_op jit(solution)/shard_map/ppermute | solution.py:20
  187.3 7.3 %collective-permute-start.29 = (f32[4,1,32,128]{3,2,1,0:T(8,128)S(1)}, f32[4,1,32,128]{3,2,1,0:T(8,128)S(1)}, u32[]{:S(2)}, u32[]{:S(2)}) collective-permute-start(f32[4,1,32,128]{3,2,1,0:T(8,128)S(1)} %get-tuple-element.139), channel_id=1, source_target_pairs={{4,0},{8,4},{12,8},{16,12},{20,16},{24,20},{28,24},{32,28},{36,32}... | collective-permute-start | bytes 196616 | tf_op jit(solution)/shard_map/ppermute | solution.py:23
  188.6 6.0 %collective-permute-start.28 = (f32[4,1,32,128]{3,2,1,0:T(8,128)S(1)}, f32[4,1,32,128]{3,2,1,0:T(8,128)S(1)}, u32[]{:S(2)}, u32[]{:S(2)}) collective-permute-start(f32[4,1,32,128]{3,2,1,0:T(8,128)S(1)} %get-tuple-element.138), channel_id=1, source_target_pairs={{0,4},{4,8},{8,12},{12,16},{16,20},{20,24},{24,28},{28,32},{32,36}... | collective-permute-start | bytes 196616 | tf_op jit(solution)/shard_map/ppermute | solution.py:20
  194.7 16.0 %collective-permute-start.31 = (f32[4,6,1,128]{3,2,1,0:T(1,128)S(1)}, f32[4,6,1,128]{3,2,1,0:T(1,128)S(1)}, u32[]{:S(2)}, u32[]{:S(2)}) collective-permute-start(f32[4,6,1,128]{3,2,1,0:T(1,128)S(1)} %get-tuple-element.109), channel_id=1, source_target_pairs={{1,0},{2,1},{3,2},{5,4},{6,5},{7,6},{9,8},{10,9},{11,10},{13,12},{... | collective-permute-start | bytes 36872 | tf_op jit(solution)/shard_map/ppermute | solution.py:23
  196.6 14.0 %collective-permute-start.30 = (f32[4,6,1,128]{3,2,1,0:T(1,128)S(1)}, f32[4,6,1,128]{3,2,1,0:T(1,128)S(1)}, u32[]{:S(2)}, u32[]{:S(2)}) collective-permute-start(f32[4,6,1,128]{3,2,1,0:T(1,128)S(1)} %get-tuple-element.108), channel_id=1, source_target_pairs={{0,1},{1,2},{2,3},{4,5},{5,6},{6,7},{8,9},{9,10},{10,11},{12,13},{... | collective-permute-start | bytes 36872 | tf_op jit(solution)/shard_map/ppermute | solution.py:20
  202.7 53.5 %collective-permute-start.35 = (f32[4,6,1,128]{3,2,1,0:T(1,128)S(1)}, f32[4,6,1,128]{3,2,1,0:T(1,128)S(1)}, u32[]{:S(2)}, u32[]{:S(2)}) collective-permute-start(f32[4,6,1,128]{3,2,1,0:T(1,128)S(1)} %get-tuple-element.107), channel_id=1, source_target_pairs={{1,0},{2,1},{3,2},{5,4},{6,5},{7,6},{9,8},{10,9},{11,10},{13,12},{... | collective-permute-start | bytes 36872 | tf_op jit(solution)/shard_map/ppermute | solution.py:23
  204.6 51.5 %collective-permute-start.34 = (f32[4,6,1,128]{3,2,1,0:T(1,128)S(1)}, f32[4,6,1,128]{3,2,1,0:T(1,128)S(1)}, u32[]{:S(2)}, u32[]{:S(2)}) collective-permute-start(f32[4,6,1,128]{3,2,1,0:T(1,128)S(1)} %get-tuple-element.106), channel_id=1, source_target_pairs={{0,1},{1,2},{2,3},{4,5},{5,6},{6,7},{8,9},{9,10},{10,11},{12,13},{... | collective-permute-start | bytes 36872 | tf_op jit(solution)/shard_map/ppermute | solution.py:20
  257.3 4.3 collective-permute-start.37
  258.6 3.9 collective-permute-start.36
  262.6 8.0 %collective-permute-start.39 = (f32[4,6,1,128]{3,2,1,0:T(1,128)S(1)}, f32[4,6,1,128]{3,2,1,0:T(1,128)S(1)}, u32[]{:S(2)}, u32[]{:S(2)}) collective-permute-start(f32[4,6,1,128]{3,2,1,0:T(1,128)S(1)} %get-tuple-element.105), channel_id=1, source_target_pairs={{1,0},{2,1},{3,2},{5,4},{6,5},{7,6},{9,8},{10,9},{11,10},{13,12},{... | collective-permute-start | bytes 36872 | tf_op jit(solution)/shard_map/ppermute | solution.py:23
  266.9 6.5 %collective-permute-start.38 = (f32[4,6,1,128]{3,2,1,0:T(1,128)S(1)}, f32[4,6,1,128]{3,2,1,0:T(1,128)S(1)}, u32[]{:S(2)}, u32[]{:S(2)}) collective-permute-start(f32[4,6,1,128]{3,2,1,0:T(1,128)S(1)} %get-tuple-element.104), channel_id=1, source_target_pairs={{0,1},{1,2},{2,3},{4,5},{5,6},{6,7},{8,9},{9,10},{10,11},{12,13},{... | collective-permute-start | bytes 36872 | tf_op jit(solution)/shard_map/ppermute | solution.py:20
  273.7 4.3 collective-permute-start.41
  279.0 8.0 %collective-permute-start.43 = (f32[4,6,1,128]{3,2,1,0:T(1,128)S(1)}, f32[4,6,1,128]{3,2,1,0:T(1,128)S(1)}, u32[]{:S(2)}, u32[]{:S(2)}) collective-permute-start(f32[4,6,1,128]{3,2,1,0:T(1,128)S(1)} %get-tuple-element.103), channel_id=1, source_target_pairs={{1,0},{2,1},{3,2},{5,4},{6,5},{7,6},{9,8},{10,9},{11,10},{13,12},{... | collective-permute-start | bytes 36872 | tf_op jit(solution)/shard_map/ppermute | solution.py:23
  280.9 7.4 %collective-permute-start.42 = (f32[4,6,1,128]{3,2,1,0:T(1,128)S(1)}, f32[4,6,1,128]{3,2,1,0:T(1,128)S(1)}, u32[]{:S(2)}, u32[]{:S(2)}) collective-permute-start(f32[4,6,1,128]{3,2,1,0:T(1,128)S(1)} %get-tuple-element.102), channel_id=1, source_target_pairs={{0,1},{1,2},{2,3},{4,5},{5,6},{6,7},{8,9},{9,10},{10,11},{12,13},{... | collective-permute-start | bytes 36872 | tf_op jit(solution)/shard_map/ppermute | solution.py:20
  288.6 6.3 %collective-permute-start.45 = (f32[4,1,32,128]{3,2,1,0:T(8,128)S(1)}, f32[4,1,32,128]{3,2,1,0:T(8,128)S(1)}, u32[]{:S(2)}, u32[]{:S(2)}) collective-permute-start(f32[4,1,32,128]{3,2,1,0:T(8,128)S(1)} %get-tuple-element.131), channel_id=1, source_target_pairs={{4,0},{8,4},{12,8},{16,12},{20,16},{24,20},{28,24},{32,28},{36,32}... | collective-permute-start | bytes 196616 | tf_op jit(solution)/shard_map/ppermute | solution.py:23
  289.9 5.7 %collective-permute-start.44 = (f32[4,1,32,128]{3,2,1,0:T(8,128)S(1)}, f32[4,1,32,128]{3,2,1,0:T(8,128)S(1)}, u32[]{:S(2)}, u32[]{:S(2)}) collective-permute-start(f32[4,1,32,128]{3,2,1,0:T(8,128)S(1)} %get-tuple-element.130), channel_id=1, source_target_pairs={{0,4},{4,8},{8,12},{12,16},{16,20},{20,24},{24,28},{28,32},{32,36}... | collective-permute-start | bytes 196616 | tf_op jit(solution)/shard_map/ppermute | solution.py:20
  295.7 8.0 %collective-permute-start.47 = (f32[4,6,1,128]{3,2,1,0:T(1,128)S(1)}, f32[4,6,1,128]{3,2,1,0:T(1,128)S(1)}, u32[]{:S(2)}, u32[]{:S(2)}) collective-permute-start(f32[4,6,1,128]{3,2,1,0:T(1,128)S(1)} %get-tuple-element.101), channel_id=1, source_target_pairs={{1,0},{2,1},{3,2},{5,4},{6,5},{7,6},{9,8},{10,9},{11,10},{13,12},{... | collective-permute-start | bytes 36872 | tf_op jit(solution)/shard_map/ppermute | solution.py:23
  297.6 7.4 %collective-permute-start.46 = (f32[4,6,1,128]{3,2,1,0:T(1,128)S(1)}, f32[4,6,1,128]{3,2,1,0:T(1,128)S(1)}, u32[]{:S(2)}, u32[]{:S(2)}) collective-permute-start(f32[4,6,1,128]{3,2,1,0:T(1,128)S(1)} %get-tuple-element.100), channel_id=1, source_target_pairs={{0,1},{1,2},{2,3},{4,5},{5,6},{6,7},{8,9},{9,10},{10,11},{12,13},{... | collective-permute-start | bytes 36872 | tf_op jit(solution)/shard_map/ppermute | solution.py:20
  305.3 7.3 %collective-permute-start.49 = (f32[4,1,32,128]{3,2,1,0:T(8,128)S(1)}, f32[4,1,32,128]{3,2,1,0:T(8,128)S(1)}, u32[]{:S(2)}, u32[]{:S(2)}) collective-permute-start(f32[4,1,32,128]{3,2,1,0:T(8,128)S(1)} %get-tuple-element.129), channel_id=1, source_target_pairs={{4,0},{8,4},{12,8},{16,12},{20,16},{24,20},{28,24},{32,28},{36,32}... | collective-permute-start | bytes 196616 | tf_op jit(solution)/shard_map/ppermute | solution.py:23
  306.6 6.9 %collective-permute-start.48 = (f32[4,1,32,128]{3,2,1,0:T(8,128)S(1)}, f32[4,1,32,128]{3,2,1,0:T(8,128)S(1)}, u32[]{:S(2)}, u32[]{:S(2)}) collective-permute-start(f32[4,1,32,128]{3,2,1,0:T(8,128)S(1)} %get-tuple-element.128), channel_id=1, source_target_pairs={{0,4},{4,8},{8,12},{12,16},{16,20},{20,24},{24,28},{28,32},{32,36}... | collective-permute-start | bytes 196616 | tf_op jit(solution)/shard_map/ppermute | solution.py:20
  313.5 8.0 %collective-permute-start.51 = (f32[4,6,1,128]{3,2,1,0:T(1,128)S(1)}, f32[4,6,1,128]{3,2,1,0:T(1,128)S(1)}, u32[]{:S(2)}, u32[]{:S(2)}) collective-permute-start(f32[4,6,1,128]{3,2,1,0:T(1,128)S(1)} %get-tuple-element.99), channel_id=1, source_target_pairs={{1,0},{2,1},{3,2},{5,4},{6,5},{7,6},{9,8},{10,9},{11,10},{13,12},{... | collective-permute-start | bytes 36872 | tf_op jit(solution)/shard_map/ppermute | solution.py:23
  315.5 7.4 %collective-permute-start.50 = (f32[4,6,1,128]{3,2,1,0:T(1,128)S(1)}, f32[4,6,1,128]{3,2,1,0:T(1,128)S(1)}, u32[]{:S(2)}, u32[]{:S(2)}) collective-permute-start(f32[4,6,1,128]{3,2,1,0:T(1,128)S(1)} %get-tuple-element.98), channel_id=1, source_target_pairs={{0,1},{1,2},{2,3},{4,5},{5,6},{6,7},{8,9},{9,10},{10,11},{12,13},{... | collective-permute-start | bytes 36872 | tf_op jit(solution)/shard_map/ppermute | solution.py:20
  323.2 6.9 %collective-permute-start.53 = (f32[4,1,32,128]{3,2,1,0:T(8,128)S(1)}, f32[4,1,32,128]{3,2,1,0:T(8,128)S(1)}, u32[]{:S(2)}, u32[]{:S(2)}) collective-permute-start(f32[4,1,32,128]{3,2,1,0:T(8,128)S(1)} %get-tuple-element.127), channel_id=1, source_target_pairs={{4,0},{8,4},{12,8},{16,12},{20,16},{24,20},{28,24},{32,28},{36,32}... | collective-permute-start | bytes 196616 | tf_op jit(solution)/shard_map/ppermute | solution.py:23
  324.5 6.5 %collective-permute-start.52 = (f32[4,1,32,128]{3,2,1,0:T(8,128)S(1)}, f32[4,1,32,128]{3,2,1,0:T(8,128)S(1)}, u32[]{:S(2)}, u32[]{:S(2)}) collective-permute-start(f32[4,1,32,128]{3,2,1,0:T(8,128)S(1)} %get-tuple-element.126), channel_id=1, source_target_pairs={{0,4},{4,8},{8,12},{12,16},{16,20},{20,24},{24,28},{28,32},{32,36}... | collective-permute-start | bytes 196616 | tf_op jit(solution)/shard_map/ppermute | solution.py:20
  331.0 8.0 %collective-permute-start.55 = (f32[4,6,1,128]{3,2,1,0:T(1,128)S(1)}, f32[4,6,1,128]{3,2,1,0:T(1,128)S(1)}, u32[]{:S(2)}, u32[]{:S(2)}) collective-permute-start(f32[4,6,1,128]{3,2,1,0:T(1,128)S(1)} %get-tuple-element.97), channel_id=1, source_target_pairs={{1,0},{2,1},{3,2},{5,4},{6,5},{7,6},{9,8},{10,9},{11,10},{13,12},{... | collective-permute-start | bytes 36872 | tf_op jit(solution)/shard_map/ppermute | solution.py:23
  332.9 7.4 %collective-permute-start.54 = (f32[4,6,1,128]{3,2,1,0:T(1,128)S(1)}, f32[4,6,1,128]{3,2,1,0:T(1,128)S(1)}, u32[]{:S(2)}, u32[]{:S(2)}) collective-permute-start(f32[4,6,1,128]{3,2,1,0:T(1,128)S(1)} %get-tuple-element.96), channel_id=1, source_target_pairs={{0,1},{1,2},{2,3},{4,5},{5,6},{6,7},{8,9},{9,10},{10,11},{12,13},{... | collective-permute-start | bytes 36872 | tf_op jit(solution)/shard_map/ppermute | solution.py:20
  340.7 6.9 %collective-permute-start.57 = (f32[4,1,32,128]{3,2,1,0:T(8,128)S(1)}, f32[4,1,32,128]{3,2,1,0:T(8,128)S(1)}, u32[]{:S(2)}, u32[]{:S(2)}) collective-permute-start(f32[4,1,32,128]{3,2,1,0:T(8,128)S(1)} %get-tuple-element.125), channel_id=1, source_target_pairs={{4,0},{8,4},{12,8},{16,12},{20,16},{24,20},{28,24},{32,28},{36,32}... | collective-permute-start | bytes 196616 | tf_op jit(solution)/shard_map/ppermute | solution.py:23
  342.0 6.5 %collective-permute-start.56 = (f32[4,1,32,128]{3,2,1,0:T(8,128)S(1)}, f32[4,1,32,128]{3,2,1,0:T(8,128)S(1)}, u32[]{:S(2)}, u32[]{:S(2)}) collective-permute-start(f32[4,1,32,128]{3,2,1,0:T(8,128)S(1)} %get-tuple-element.124), channel_id=1, source_target_pairs={{0,4},{4,8},{8,12},{12,16},{16,20},{20,24},{24,28},{28,32},{32,36}... | collective-permute-start | bytes 196616 | tf_op jit(solution)/shard_map/ppermute | solution.py:20
  348.5 8.0 %collective-permute-start.59 = (f32[4,6,1,128]{3,2,1,0:T(1,128)S(1)}, f32[4,6,1,128]{3,2,1,0:T(1,128)S(1)}, u32[]{:S(2)}, u32[]{:S(2)}) collective-permute-start(f32[4,6,1,128]{3,2,1,0:T(1,128)S(1)} %get-tuple-element.95), channel_id=1, source_target_pairs={{1,0},{2,1},{3,2},{5,4},{6,5},{7,6},{9,8},{10,9},{11,10},{13,12},{... | collective-permute-start | bytes 36872 | tf_op jit(solution)/shard_map/ppermute | solution.py:23
  350.4 7.4 %collective-permute-start.58 = (f32[4,6,1,128]{3,2,1,0:T(1,128)S(1)}, f32[4,6,1,128]{3,2,1,0:T(1,128)S(1)}, u32[]{:S(2)}, u32[]{:S(2)}) collective-permute-start(f32[4,6,1,128]{3,2,1,0:T(1,128)S(1)} %get-tuple-element.94), channel_id=1, source_target_pairs={{0,1},{1,2},{2,3},{4,5},{5,6},{6,7},{8,9},{9,10},{10,11},{12,13},{... | collective-permute-start | bytes 36872 | tf_op jit(solution)/shard_map/ppermute | solution.py:20
  358.3 7.1 %collective-permute-start.61 = (f32[8,1,32,128]{3,2,1,0:T(8,128)S(1)}, f32[8,1,32,128]{3,2,1,0:T(8,128)S(1)}, u32[]{:S(2)}, u32[]{:S(2)}) collective-permute-start(f32[8,1,32,128]{3,2,1,0:T(8,128)S(1)} %get-tuple-element.91), channel_id=1, source_target_pairs={{4,0},{8,4},{12,8},{16,12},{20,16},{24,20},{28,24},{32,28},{36,32}... | collective-permute-start | bytes 393224 | tf_op jit(solution)/shard_map/ppermute | solution.py:23
  359.6 6.7 %collective-permute-start.60 = (f32[8,1,32,128]{3,2,1,0:T(8,128)S(1)}, f32[8,1,32,128]{3,2,1,0:T(8,128)S(1)}, u32[]{:S(2)}, u32[]{:S(2)}) collective-permute-start(f32[8,1,32,128]{3,2,1,0:T(8,128)S(1)} %get-tuple-element.90), channel_id=1, source_target_pairs={{0,4},{4,8},{8,12},{12,16},{16,20},{20,24},{24,28},{28,32},{32,36}... | collective-permute-start | bytes 393224 | tf_op jit(solution)/shard_map/ppermute | solution.py:20
  366.4 8.8 %collective-permute-start.63 = (f32[8,6,1,128]{3,2,1,0:T(1,128)S(1)}, f32[8,6,1,128]{3,2,1,0:T(1,128)S(1)}, u32[]{:S(2)}, u32[]{:S(2)}) collective-permute-start(f32[8,6,1,128]{3,2,1,0:T(1,128)S(1)} %get-tuple-element.83), channel_id=1, source_target_pairs={{1,0},{2,1},{3,2},{5,4},{6,5},{7,6},{9,8},{10,9},{11,10},{13,12},{... | collective-permute-start | bytes 73736 | tf_op jit(solution)/shard_map/ppermute | solution.py:23
  368.4 7.5 %collective-permute-start.62 = (f32[8,6,1,128]{3,2,1,0:T(1,128)S(1)}, f32[8,6,1,128]{3,2,1,0:T(1,128)S(1)}, u32[]{:S(2)}, u32[]{:S(2)}) collective-permute-start(f32[8,6,1,128]{3,2,1,0:T(1,128)S(1)} %get-tuple-element.82), channel_id=1, source_target_pairs={{0,1},{1,2},{2,3},{4,5},{5,6},{6,7},{8,9},{9,10},{10,11},{12,13},{... | collective-permute-start | bytes 73736 | tf_op jit(solution)/shard_map/ppermute | solution.py:20
  (22 other events, 410.6 us)
Sparse Core Ops, SparseCore 0:
  377.1 100.5 all-reduce.20
